TPU v7x, 128 devices: a whole 4x4x4 slice. The times are simulated.
128 devices in a mesh: section: 32 (over z, x, core), dp: 4 (over y).
Axes of the slice: x: 4, y: 4, z: 4, core: 2. Of those that a mesh axis runs over, the one named last changes fastest.
Arguments:
- video_ids: int32 [32, 32], P('dp'), may hold values from 0 to 1023
- action_ids: int32 [32, 32], P('dp'), may hold values from 0 to 7
- target_ids: int32 [32, 32], P('dp'), may hold values from 0 to 1023
- live_lengths: int32 [4, 8], P('dp'), may hold values from 1 to 32, 160 in all within a row
- video_table: bfloat16 [1024, 2048], replicated, may hold values from -25 to 25
- action_table: bfloat16 [8, 2048], replicated, may hold values from -6 to 6
- layer_gain: float32 [32, 2048], P('section'), may hold values from 0.1 to 1.9
- layer_weight: bfloat16 [32, 2048, 2048], P('section', 'dp'), may hold values from -0.125 to 0.125
- out_gain: float32 [2048], replicated, may hold values from 0.1 to 1.9
- head_weight: bfloat16 [2048, 1024], replicated, may hold values from -32 to 32
Outputs:
- loss: float32 [], replicated
- weight_grad: float32 [32, 2048, 2048], P('section', 'dp')
Inputs may be any that keep to these rules, and one draw needn't show every extreme that they name: Each row of live_lengths sums to 160.
All inputs are finite; a program needn't handle non-finite values.
Results may differ from a plain program's by a relative error of at most 0.015.
Values may be sent and summed in bfloat16 or wider, within the bound.
A program may use at most 128 MiB of HBM per device.

v0:
```python
import jax
import jax.numpy as jnp
from jax import lax
from jax.sharding import PartitionSpec as P


def passed_along(block, axis, distance):
    devices = range(lax.axis_size(axis))
    route = [(i - distance, i) for i in devices if i - distance in devices]
    return lax.ppermute(block, axis, route)


def norm_rows(hidden, scale_vector):
    widened = hidden.astype(jnp.float32)
    inverse = lax.rsqrt(jnp.mean(widened * widened, axis=-1, keepdims=True) + 1e-05)
    return widened * inverse * scale_vector


def contract_rows(left, right):
    return lax.dot_general(
        left, right, (((0,), (0,)), ((), ())), preferred_element_type=jnp.float32
    )


def times_transpose(left, right):
    return lax.dot_general(
        left, right, (((1,), (1,)), ((), ())), preferred_element_type=jnp.float32
    )


def layer_forward(hidden, scale_vector, weight):
    normed = norm_rows(hidden, scale_vector).astype(jnp.bfloat16)
    pre_act = jnp.dot(normed, weight, preferred_element_type=jnp.float32)
    result = (hidden.astype(jnp.float32) + jax.nn.gelu(pre_act)).astype(jnp.bfloat16)
    return (result, normed, pre_act)


def layer_backward(hidden, scale_vector, weight, pre_act, cotangent):
    widened = cotangent.astype(jnp.float32)
    _, gelu_back = jax.vjp(jax.nn.gelu, pre_act)
    d_pre = gelu_back(widened)[0].astype(jnp.bfloat16)
    d_normed = times_transpose(d_pre, weight)
    _, norm_back = jax.vjp(
        lambda rows_in: norm_rows(rows_in, scale_vector), hidden.astype(jnp.float32)
    )
    d_hidden = (widened + norm_back(d_normed)[0]).astype(jnp.bfloat16)
    return (d_hidden, d_pre)


def head_terms(final_rows, out_gain, head_weight, targets, live_mask):
    normed = norm_rows(final_rows, out_gain).astype(jnp.bfloat16)
    logits = jnp.dot(normed, head_weight, preferred_element_type=jnp.float32)
    row_max = jnp.max(logits, axis=-1, keepdims=True)
    exponents = jnp.exp(logits - row_max)
    denominator = jnp.sum(exponents, axis=-1, keepdims=True)
    one_hot = (targets[:, None] == lax.broadcasted_iota(jnp.int32, logits.shape, 1)).astype(
        jnp.float32
    )
    picked = jnp.sum(logits * one_hot, axis=-1)
    losses = (jnp.log(denominator[:, 0]) + row_max[:, 0] - picked) * live_mask
    d_logits = ((exponents / denominator - one_hot) * live_mask[:, None]).astype(jnp.bfloat16)
    d_normed = times_transpose(d_logits, head_weight)
    _, norm_back = jax.vjp(
        lambda rows_in: norm_rows(rows_in, out_gain), final_rows.astype(jnp.float32)
    )
    d_final = norm_back(d_normed)[0].astype(jnp.bfloat16)
    return (jnp.sum(losses), jnp.sum(live_mask), d_final)


def put_block(stored, value, current):
    return lax.dynamic_update_index_in_dim(stored, value, current, 0)


def take_block(stored, current):
    return lax.dynamic_index_in_dim(stored, current, 0, False)


def shards(
    video_ids,
    action_ids,
    target_ids,
    live_lengths,
    video_table,
    action_table,
    layer_gain,
    layer_weight,
    out_gain,
    head_weight,
):
    section_count = lax.axis_size("section")
    section_index = lax.axis_index("section")
    final_section = section_count - 1
    weight = lax.all_gather(layer_weight[0], "dp", axis=0, tiled=True)
    scale_vector = layer_gain[0]
    micro_count, tokens_each = video_ids.shape
    model_width = weight.shape[1]
    embedded = (
        jnp.take(video_table, video_ids, axis=0).astype(jnp.float32)
        + jnp.take(action_table, action_ids, axis=0).astype(jnp.float32)
    ).astype(jnp.bfloat16)
    positions = lax.broadcasted_iota(jnp.int32, (micro_count, tokens_each), 1)
    live_mask = (positions < live_lengths[0][:, None]).astype(jnp.float32).reshape(-1)
    targets = target_ids.reshape(-1)
    ticks = micro_count + section_count - 1
    blank_rows = jnp.zeros((micro_count, tokens_each, model_width), jnp.bfloat16)
    blank_wide = jnp.zeros((micro_count, tokens_each, model_width), jnp.float32)
    blank_block = jnp.zeros((tokens_each, model_width), jnp.bfloat16)

    def forward_tick(step_index, carry):
        incoming = carry[0]
        current = step_index - section_index
        active = jnp.logical_and(current >= 0, current < micro_count)
        current = jnp.clip(current, 0, micro_count - 1)
        hidden = jnp.where(section_index == 0, take_block(embedded, current), incoming)

        def forward_run_layer(stored):
            result, normed, pre_act = layer_forward(hidden, scale_vector, weight)
            kept_in, kept_norm, kept_pre, finals = stored
            return (
                result,
                (
                    put_block(kept_in, hidden, current),
                    put_block(kept_norm, normed, current),
                    put_block(kept_pre, pre_act, current),
                    put_block(finals, result, current),
                ),
            )

        def forward_pass_over(stored):
            return (blank_block, stored)

        result, stored = lax.cond(active, forward_run_layer, forward_pass_over, carry[1:])
        incoming = passed_along(result, "section", 1)
        return (incoming,) + stored

    forward_init = (blank_block, blank_rows, blank_rows, blank_wide, blank_rows)
    _, kept_in, kept_norm, kept_pre, finals = lax.fori_loop(0, ticks, forward_tick, forward_init)

    def head_run(final_rows):
        return head_terms(final_rows, out_gain, head_weight, targets, live_mask)

    def head_skip(final_rows):
        return (jnp.zeros((), jnp.float32), jnp.zeros((), jnp.float32), jnp.zeros_like(final_rows))

    loss_sum, live_count, d_final = lax.cond(
        section_index == final_section,
        head_run,
        head_skip,
        finals.reshape(micro_count * tokens_each, model_width),
    )
    d_final = d_final.reshape(micro_count, tokens_each, model_width)
    loss_sum, live_count = lax.psum((loss_sum, live_count), ("section", "dp"))
    loss = loss_sum / live_count

    def add_product(running, normed, d_pre):
        return running + contract_rows(normed, d_pre)

    holding = jnp.zeros((model_width, model_width), jnp.float32)

    def backward_tick(step_index, carry):
        incoming, holding = carry
        current = step_index - (final_section - section_index)
        active = jnp.logical_and(current >= 0, current < micro_count)
        current = jnp.clip(current, 0, micro_count - 1)
        cotangent = jnp.where(
            section_index == final_section, take_block(d_final, current), incoming
        )

        def backward_run_layer(holding):
            normed = take_block(kept_norm, current)
            d_hidden, d_pre = layer_backward(
                take_block(kept_in, current),
                scale_vector,
                weight,
                take_block(kept_pre, current),
                cotangent,
            )
            return (d_hidden, add_product(holding, normed, d_pre))

        def backward_pass_over(holding):
            return (blank_block, holding)

        d_hidden, holding = lax.cond(active, backward_run_layer, backward_pass_over, holding)
        incoming = passed_along(d_hidden, "section", -1)
        return (incoming, holding)

    running = lax.fori_loop(0, ticks, backward_tick, (blank_block, holding))[1]
    grad_share = lax.psum_scatter(
        running.astype(jnp.bfloat16), "dp", scatter_dimension=0, tiled=True
    ).astype(jnp.float32)
    return (loss, grad_share[None])


def solution(mesh):
    in_specs = (
        P("dp", None),
        P("dp", None),
        P("dp", None),
        P("dp", None),
        P(),
        P(),
        P("section", None),
        P("section", "dp", None),
        P(),
        P(),
    )
    out_specs = (P(), P("section", "dp", None))
    return jax.shard_map(shards, mesh=mesh, in_specs=in_specs, out_specs=out_specs, check_vma=False)
```

profile of v0, /device:TPU:0, one launch (start us, length us, event | category | flops | bytes accessed | tf_op | source)
XLA Modules:
  0.0 1720.0 jit_solution(11400610913832479152)
XLA Ops:
  16.2 79.1 %all-gather.3.cloned.1.call-done = bf16[1,2048,2048]{2,1,0:T(8,128)(2,1)} async-done(((bf16[1,512,2048]{2,1,0:T(8,128)(2,1)}), bf16[1,2048,2048]{2,1,0:T(8,128)(2,1)}) %all-gather.3.cloned.1.call-update) | async-done | bytes 8388624 | tf_op jit(solution)/shard_map/all_gather | solution.py:93
  98.0 378.7 %while.42 = (s32[]{:T(128)}, bf16[32,2048]{1,0:T(8,128)(2,1)S(1)}, bf16[8,32,2048]{2,1,0:T(8,128)(2,1)}, bf16[8,32,2048]{2,1,0:T(8,128)(2,1)}, f32[8,32,2048]{2,...) while((s32[]{:T(128)}, bf16[32,2048]{1,0:T(8,128)(2,1)S(1)}, ...), condition=%wide.region_4.5_spmd, body=%wide.region_0.4_spmd.sunk | while | flops 269877280 | bytes 11028751 | solution.py:137
  218.0 12.7 collective-permute-start
  301.9 14.8 collective-permute-start
  326.1 14.8 collective-permute-start
  485.7 1134.4 %while.43 = (s32[]{:T(128)}, bf16[32,2048]{1,0:T(8,128)(2,1)S(1)}, f32[2048,2048]{1,0:T(8,128)}, s32[]{:T(128)}, pred[]{:T(512)}, /*index=5*/bf16[8,32,2048]{2,1...) while((s32[]{:T(128)}, bf16[32,2048]{1,0:T(8,128)(2,1)S(1)}, ...), condition=%wide.region_21.22_spmd, body=%wide.region_16.21_spmd.sunk | while | flops 544931968 | bytes 44839248 | solution.py:187
  742.1 646.2 %collective-permute-done.1 = bf16[32,2048]{1,0:T(8,128)(2,1)S(1)} collective-permute-done((bf16[32,2048]{1,0:T(8,128)(2,1)S(1)}, bf16[32,2048]{1,0:T(8,128)(2,1)S(1)}, u32[]{:S(2)}, u32[]{:S(2)}) %collective-permute-start.1) | collective-permute-done | bytes 131104 | tf_op jit(solution)/shard_map/while/body/eval_jaxpr/ppermute | solution.py:10
  1388.3 21.2 %conditional.7 = (bf16[32,2048]{1,0:T(8,128)(2,1)S(1)}, f32[2048,2048]{1,0:T(8,128)}) conditional(s32[]{:T(128)} %convert_element_type.200, f32[2048,2048]{1,0:T(8,128)} %get-tuple-element.1037, (pred[]{:T(512)}, s32[]{:T(128)}, bf16[8,32,2048]{2,1,0:T(8,128)(2,1)}, bf16[32,2048]{1,0:T(8,128)(2,1)S(1)}, f32[8,32,2048]{2,1,0:T(8,128)S(1)}, ...), branch_computations={%region_17.17_spmd, %region_18.20_spmd} | conditional | flops 544931968 | bytes 44314668 | solution.py:183
  1395.5 14.0 convolution_add_fusion
  1417.9 21.2 %conditional.7 = (bf16[32,2048]{1,0:T(8,128)(2,1)S(1)}, f32[2048,2048]{1,0:T(8,128)}) conditional(s32[]{:T(128)} %convert_element_type.200, f32[2048,2048]{1,0:T(8,128)} %get-tuple-element.1037, (pred[]{:T(512)}, s32[]{:T(128)}, bf16[8,32,2048]{2,1,0:T(8,128)(2,1)}, bf16[32,2048]{1,0:T(8,128)(2,1)S(1)}, f32[8,32,2048]{2,1,0:T(8,128)S(1)}, ...), branch_computations={%region_17.17_spmd, %region_18.20_spmd} | conditional | flops 544931968 | bytes 44314668 | solution.py:183
  1425.1 14.0 convolution_add_fusion
  1447.5 21.2 %conditional.7 = (bf16[32,2048]{1,0:T(8,128)(2,1)S(1)}, f32[2048,2048]{1,0:T(8,128)}) conditional(s32[]{:T(128)} %convert_element_type.200, f32[2048,2048]{1,0:T(8,128)} %get-tuple-element.1037, (pred[]{:T(512)}, s32[]{:T(128)}, bf16[8,32,2048]{2,1,0:T(8,128)(2,1)}, bf16[32,2048]{1,0:T(8,128)(2,1)S(1)}, f32[8,32,2048]{2,1,0:T(8,128)S(1)}, ...), branch_computations={%region_17.17_spmd, %region_18.20_spmd} | conditional | flops 544931968 | bytes 44314668 | solution.py:183
  1454.7 14.0 convolution_add_fusion
  1477.1 21.2 %conditional.7 = (bf16[32,2048]{1,0:T(8,128)(2,1)S(1)}, f32[2048,2048]{1,0:T(8,128)}) conditional(s32[]{:T(128)} %convert_element_type.200, f32[2048,2048]{1,0:T(8,128)} %get-tuple-element.1037, (pred[]{:T(512)}, s32[]{:T(128)}, bf16[8,32,2048]{2,1,0:T(8,128)(2,1)}, bf16[32,2048]{1,0:T(8,128)(2,1)S(1)}, f32[8,32,2048]{2,1,0:T(8,128)S(1)}, ...), branch_computations={%region_17.17_spmd, %region_18.20_spmd} | conditional | flops 544931968 | bytes 44314668 | solution.py:183
  1484.4 14.0 convolution_add_fusion
  1506.8 21.2 %conditional.7 = (bf16[32,2048]{1,0:T(8,128)(2,1)S(1)}, f32[2048,2048]{1,0:T(8,128)}) conditional(s32[]{:T(128)} %convert_element_type.200, f32[2048,2048]{1,0:T(8,128)} %get-tuple-element.1037, (pred[]{:T(512)}, s32[]{:T(128)}, bf16[8,32,2048]{2,1,0:T(8,128)(2,1)}, bf16[32,2048]{1,0:T(8,128)(2,1)S(1)}, f32[8,32,2048]{2,1,0:T(8,128)S(1)}, ...), branch_computations={%region_17.17_spmd, %region_18.20_spmd} | conditional | flops 544931968 | bytes 44314668 | solution.py:183
  1514.0 14.0 convolution_add_fusion
  1536.4 21.2 %conditional.7 = (bf16[32,2048]{1,0:T(8,128)(2,1)S(1)}, f32[2048,2048]{1,0:T(8,128)}) conditional(s32[]{:T(128)} %convert_element_type.200, f32[2048,2048]{1,0:T(8,128)} %get-tuple-element.1037, (pred[]{:T(512)}, s32[]{:T(128)}, bf16[8,32,2048]{2,1,0:T(8,128)(2,1)}, bf16[32,2048]{1,0:T(8,128)(2,1)S(1)}, f32[8,32,2048]{2,1,0:T(8,128)S(1)}, ...), branch_computations={%region_17.17_spmd, %region_18.20_spmd} | conditional | flops 544931968 | bytes 44314668 | solution.py:183
  1543.6 14.0 convolution_add_fusion
  1566.0 21.2 %conditional.7 = (bf16[32,2048]{1,0:T(8,128)(2,1)S(1)}, f32[2048,2048]{1,0:T(8,128)}) conditional(s32[]{:T(128)} %convert_element_type.200, f32[2048,2048]{1,0:T(8,128)} %get-tuple-element.1037, (pred[]{:T(512)}, s32[]{:T(128)}, bf16[8,32,2048]{2,1,0:T(8,128)(2,1)}, bf16[32,2048]{1,0:T(8,128)(2,1)S(1)}, f32[8,32,2048]{2,1,0:T(8,128)S(1)}, ...), branch_computations={%region_17.17_spmd, %region_18.20_spmd} | conditional | flops 544931968 | bytes 44314668 | solution.py:183
  1573.2 14.0 convolution_add_fusion
  1595.6 21.2 %conditional.7 = (bf16[32,2048]{1,0:T(8,128)(2,1)S(1)}, f32[2048,2048]{1,0:T(8,128)}) conditional(s32[]{:T(128)} %convert_element_type.200, f32[2048,2048]{1,0:T(8,128)} %get-tuple-element.1037, (pred[]{:T(512)}, s32[]{:T(128)}, bf16[8,32,2048]{2,1,0:T(8,128)(2,1)}, bf16[32,2048]{1,0:T(8,128)(2,1)S(1)}, f32[8,32,2048]{2,1,0:T(8,128)S(1)}, ...), branch_computations={%region_17.17_spmd, %region_18.20_spmd} | conditional | flops 544931968 | bytes 44314668 | solution.py:183
  1602.9 14.0 convolution_add_fusion
  1629.2 67.8 %all-reduce = (f32[]{:T(128)}, f32[]{:T(128)}) all-reduce(f32[]{:T(128)} %get-tuple-element.727, f32[]{:T(128)} %get-tuple-element.728), channel_id=1, replica_groups=mesh['section'=32,'dp'=4] {'section','dp'}, use_global_device_ids=true, to_apply=%region_14.15 | all-reduce | flops 2 | bytes 16 | tf_op jit(solution)/shard_map/psum | solution.py:152
  (389 shorter events, 815.0 us)
Async XLA Ops:
  7.2 88.1 %all-gather.3.cloned.1.call-start = ((), (), s32[]{:S(2)}) async-start(), calls=%async_computation.2 | async-start | bytes 10485760 | tf_op jit(solution)/shard_map/all_gather | solution.py:93
  7.9 1700.0 %reduce-scatter.2.cloned.1.call-start = ((), (), s32[]{:S(2)}) async-start(), calls=%async_computation.1 | async-start | bytes 10485760 | tf_op jit(solution)/shard_map/reduce_scatter | solution.py:188
  198.0 13.6 collective-permute-start
  218.0 13.6 collective-permute-start
  251.5 11.2 collective-permute-start
  282.7 11.2 collective-permute-start
  301.9 15.7 collective-permute-start
  317.7 8.4 collective-permute-start
  326.1 15.7 collective-permute-start
  341.9 8.4 collective-permute-start
  350.3 8.4 collective-permute-start
  358.8 8.4 collective-permute-start
  367.2 8.4 collective-permute-start
  375.6 8.4 collective-permute-start
  384.1 8.4 collective-permute-start
  392.5 8.4 collective-permute-start
  400.9 8.4 collective-permute-start
  443.1 8.4 collective-permute-start
  451.5 8.4 collective-permute-start
  494.1 9.1 collective-permute-start.1
  511.5 9.1 collective-permute-start.1
  528.9 9.1 collective-permute-start.1
  546.3 9.1 collective-permute-start.1
  740.8 647.5 %collective-permute-start.1 = (bf16[32,2048]{1,0:T(8,128)(2,1)S(1)}, bf16[32,2048]{1,0:T(8,128)(2,1)S(1)}, u32[]{:S(2)}, u32[]{:S(2)}) collective-permute-start(bf16[32,2048]{1,0:T(8,128)(2,1)S(1)} %get-tuple-element.957), channel_id=1, source_target_pairs={{4,0},{8,4},{12,8},{16,12},{20,16},{24,20},{28,24},{32,28},{36,32}... | collective-permute-start | bytes 393224 | tf_op jit(solution)/shard_map/while/body/eval_jaxpr/ppermute | solution.py:10
  (63 other events, 1192.6 us)
Sparse Core Ops, SparseCore 0:
  9.7 85.6 all-gather.2
  1629.3 78.5 reduce-scatter.1
where the time goes:
time: 1720 us
  waiting for transfers between devices  1040 us (60%)
  starting transfers between devices  331 us (19%)
  matrix products  206 us (12%)
  blocking collectives  67.8 us (4%)
  other arithmetic  37.6 us (2%)
  local copies, waits for them, and re-layouts  19.1 us (1%)
    ppermute x78, waiting for transfers between devices, passed_along(): return lax.ppermute(block, axis, route)  950 us
    ppermute x78, starting transfers between devices, passed_along(): return lax.ppermute(block, axis, route)  331 us
    dot_general x8, matrix products, contract_rows(): lax.dot_general(left, right, (((0,), (0,)), ((), ())), preferred_element_...  112 us
    all_gather x1, waiting for transfers between devices, shards(): weight = lax.all_gather(layer_weight[0], 'dp', axis=0, tiled=True)  79.1 us
    psum x1, blocking collectives, shards(): loss_sum, live_count = lax.psum((loss_sum, live_count), ('section', 'dp'))  67.8 us
    dot_general x8, matrix products, times_transpose(): lax.dot_general(left, right, (((1,), (1,)), ((), ())), preferred_element_...  48.7 us
    dot_general x8, matrix products, layer_forward(): pre_act = jnp.dot(normed, weight, preferred_element_type=jnp.float32)  44.8 us
  transfers between devices with their start and end apart: 80, of which 80 were waited for; matrix products, arithmetic and copies ran while one was open for 0% of the time, Pallas kernels for 0%

commit v1 on v0

v1 whole, which is shorter than its diff:
```python
import functools

import jax
import jax.numpy as jnp
from jax import lax
from jax.experimental import pallas as pl
from jax.experimental.pallas import tpu as pltpu
from jax.sharding import PartitionSpec as P

MESH = pl.DeviceIdType.MESH
F32 = jnp.float32
BF16 = jnp.bfloat16
ROWS = 16
CUTS = 4
PRE_SCALE = 0.7978845608028654
CUBE = 0.044715


def gelu(x):
    return 0.5 * x * (1.0 + jnp.tanh(PRE_SCALE * (x + CUBE * x * x * x)))


def gelu_slope(x):
    t = jnp.tanh(PRE_SCALE * (x + CUBE * x * x * x))
    return 0.5 * (1.0 + t) + 0.5 * x * (1.0 - t * t) * (PRE_SCALE * (1.0 + 3.0 * CUBE * x * x))


def dot(left, right):
    return jnp.dot(left, right, preferred_element_type=F32)


def row_sum(x):
    return jnp.sum(x, axis=1, keepdims=True)


def kernel(
    lengths_ref,
    ids_ref,
    gains_ref,
    out_gain_ref,
    actions_ref,
    video_ref,
    weight_ref,
    head_ref,
    loss_ref,
    normed_out,
    dpre_out,
    w,
    wt,
    hw,
    ht,
    h_in,
    h_mid,
    h_out,
    pre,
    normed,
    dpre,
    g_in,
    g_out,
    dlog,
    acc,
    slope,
    inv_keep,
    picked_ids,
    loss_part,
    loss_in,
    loss_all,
    w_send,
    w_recv,
    w_fwd_send,
    w_fwd_recv,
    local_sem,
    h_send,
    h_recv,
    g_send,
    g_recv,
    peer_send,
    peer_recv,
    n_send,
    n_recv,
    d_send,
    d_recv,
    part_send,
    part_recv,
    loss_send,
    loss_recv,
):
    s = lax.axis_index("section")
    y = lax.axis_index("dp")
    planes = lax.axis_size("section") // 2
    k = s // 2
    core = s % 2
    forward = core == 1
    backward = core == 0
    first = k == 0
    last = k == planes - 1
    not_first = k > 0
    not_last = k < planes - 1

    width = w.shape[2]
    share = width // 4
    half = share // 2
    step = width // CUTS
    count = h_in.shape[0]
    vocab = hw.shape[1]

    up, down, far = (y + 1) % 4, (y + 3) % 4, (y + 2) % 4
    peer = (2 * k + 1 - core, y)
    odd = 2 * k + 1
    even = 2 * k

    def remote(src, dst, send, recv, device):
        return pltpu.make_async_remote_copy(
            src_ref=src, dst_ref=dst, send_sem=send, recv_sem=recv, device_id=device, device_id_type=MESH
        )

    barrier = pltpu.get_barrier_semaphore()
    for other in (up, down, far):
        for c in (0, 1):
            pl.semaphore_signal(barrier, inc=1, device_id=(2 * k + c, other), device_id_type=MESH)
    pl.semaphore_signal(barrier, inc=1, device_id=peer, device_id_type=MESH)

    sections = 2 * planes
    for other in ((s + 2) % sections, (s + sections - 2) % sections):
        pl.semaphore_signal(barrier, inc=1, device_id=(other, y), device_id_type=MESH)
    pl.semaphore_wait(barrier, 9)

    def rows_of(owner, part=None):
        if part is None:
            return pl.ds(pl.multiple_of(owner * share, share), share)
        return pl.ds(pl.multiple_of(owner * share + part * half, half), half)

    def direct(layer, lane, part):
        target = up if lane == 1 else down
        return remote(
            weight_ref.at[0, part * half : (part + 1) * half, :],
            w.at[layer, rows_of(y, part), :],
            w_send.at[lane, part],
            w_recv.at[layer, lane, part],
            (odd, target),
        )

    def relay(layer, part):
        owner, target = (down, up) if part == 0 else (up, down)
        block = w.at[layer, rows_of(owner, part), :]
        return remote(block, block, w_send.at[3, 2 * layer + part], w_recv.at[layer, 3, part], (odd, target))

    def to_peer(layer, lane, owner):
        block = w.at[layer, rows_of(owner), :]
        return remote(block, block, w_fwd_send.at[layer, lane], w_fwd_recv.at[layer, lane], peer)

    def own_to_peer(layer):
        return remote(
            weight_ref.at[0], w.at[layer, rows_of(y), :], w_fwd_send.at[layer, 0], w_fwd_recv.at[layer, 0], peer
        )

    def own_local(layer):
        return pltpu.make_async_copy(weight_ref.at[0], w.at[layer, rows_of(y), :], local_sem.at[0])

    def start_own(layer):
        direct(layer, 1, 0).start()
        direct(layer, 2, 1).start()
        direct(layer, 1, 1).start()
        direct(layer, 2, 0).start()
        own_to_peer(layer).start()
        own_local(layer).start()

    @pl.when(forward)
    def _():
        start_own(1)

    @pl.when(backward)
    def _():
        start_own(0)

    @pl.when(last)
    def _():
        pltpu.make_async_copy(head_ref, hw, local_sem.at[1]).start()

    @pl.when(jnp.logical_and(first, forward))
    def _():
        pltpu.make_async_copy(video_ref, ht, local_sem.at[1]).start()

    total = count * ROWS
    slots = ids_ref.shape[2]
    place = lax.broadcasted_iota(jnp.int32, (total, slots), 0)
    lane_of = lax.broadcasted_iota(jnp.int32, (total, slots), 1)
    chosen = [jnp.zeros((total, 1), jnp.int32) for _ in range(3)]
    start = jnp.int32(0)
    for b in range(ids_ref.shape[1]):
        length = lengths_ref[0, b]
        hit = jnp.logical_and(place == start + lane_of, lane_of < length)
        for kind in range(3):
            line = jnp.broadcast_to(ids_ref[kind, b : b + 1, :], (total, slots))
            chosen[kind] = chosen[kind] + row_sum(jnp.where(hit, line, 0))
        start = start + length
    picked_ids[...] = jnp.broadcast_to(chosen[2], picked_ids.shape)

    @pl.when(jnp.logical_and(first, forward))
    def _():
        pltpu.make_async_copy(video_ref, ht, local_sem.at[1]).wait()
        video_hot = (chosen[0] == lax.broadcasted_iota(jnp.int32, (total, ht.shape[0]), 1)).astype(F32).astype(BF16)
        kinds = actions_ref.shape[0]
        for j in range(CUTS):
            cols = slice(j * step, (j + 1) * step)
            rows = dot(video_hot, ht[:, cols])
            for a in range(kinds):
                rows = rows + jnp.where(chosen[1] == a, actions_ref[a : a + 1, cols].astype(F32), 0.0)
            h_in[:, :, cols] = rows.astype(BF16).reshape(count, ROWS, step)

    @pl.when(forward)
    def _():
        for layer in range(2):
            direct(layer, 1, 0).wait_recv()
            relay(layer, 0).start()
            direct(layer, 2, 1).wait_recv()
            relay(layer, 1).start()
        for layer in range(2):
            direct(layer, 1, 1).wait_recv()
            to_peer(layer, 1, down).start()
            direct(layer, 2, 0).wait_recv()
            to_peer(layer, 2, up).start()
        for layer in range(2):
            relay(layer, 0).wait_recv()
            relay(layer, 1).wait_recv()
            to_peer(layer, 3, far).start()
        own_local(1).wait()
        own_to_peer(0).wait_recv()

    @pl.when(jnp.logical_and(last, forward))
    def _():
        pltpu.make_async_copy(head_ref, hw, local_sem.at[1]).wait()

    block = min(512, width)

    def turn(layer, owner):
        def one(i, carry):
            cols = pl.ds(pl.multiple_of(i * block, block), block)
            wt[layer, cols, rows_of(owner)] = w[layer, rows_of(owner), cols].T
            return carry

        lax.fori_loop(0, width // block, one, 0)

    @pl.when(backward)
    def _():
        own_local(0).wait()
        turn(0, y)
        own_to_peer(1).wait_recv()
        turn(1, y)
        for lane, owner in ((1, down), (2, up), (3, far)):
            for layer in range(2):
                to_peer(layer, lane, owner).wait_recv()
                turn(layer, owner)

    @pl.when(jnp.logical_and(last, backward))
    def _():
        pltpu.make_async_copy(head_ref, hw, local_sem.at[1]).wait()
        for i in range(CUTS):
            ht[:, i * step : (i + 1) * step] = hw[i * step : (i + 1) * step, :].T

    def h_piece(mb, j):
        cols = pl.ds(j * step, step)
        return remote(
            h_out.at[mb, :, cols], h_in.at[mb, :, cols], h_send.at[j], h_recv.at[mb, j], (s + 2, y)
        )

    def peer_copies(mb):
        refs = [h_in, h_mid, pre.at[0], pre.at[1]]
        return [
            remote(ref.at[mb], ref.at[mb], peer_send.at[i], peer_recv.at[i, mb], peer) for i, ref in enumerate(refs)
        ]

    def head_copies(mb):
        return [
            remote(ref.at[mb], ref.at[mb], peer_send.at[4 + i], peer_recv.at[4 + i, mb], peer)
            for i, ref in enumerate([h_out, dlog])
        ]

    def inverse(squares):
        return lax.rsqrt(squares * (1.0 / width) + 1e-05)

    def cut(j):
        return slice(j * step, (j + 1) * step)

    def forward_one(mb, carry):
        squares = jnp.zeros((ROWS, 1), F32)
        for j in range(CUTS):

            @pl.when(not_first)
            def _(j=j):
                h_piece(mb, j).wait_recv()

            h = h_in[mb, :, cut(j)].astype(F32)
            squares = squares + row_sum(h * h)
            scaled = (h * gains_ref[0:1, cut(j)]).astype(BF16)
            product = dot(scaled, w[0, cut(j), :])
            if j == 0:
                acc[...] = product
            else:
                acc[...] += product
        inv = inverse(squares)
        squares = jnp.zeros((ROWS, 1), F32)
        for j in range(CUTS):
            h = h_in[mb, :, cut(j)].astype(F32)
            at = acc[:, cut(j)] * inv
            pre[0, mb, :, cut(j)] = at
            result = (h + gelu(at)).astype(BF16)
            h_mid[mb, :, cut(j)] = result
            wide = result.astype(F32)
            squares = squares + row_sum(wide * wide)
        inv_mid = inverse(squares)
        for j in range(CUTS):
            normed[1, mb, :, cut(j)] = (
                h_mid[mb, :, cut(j)].astype(F32) * inv_mid * gains_ref[1:2, cut(j)]
            ).astype(BF16)
        squares = jnp.zeros((ROWS, 1), F32)
        for j in range(CUTS):
            at = dot(normed[1, mb], w[1, :, cut(j)])
            result = (h_mid[mb, :, cut(j)].astype(F32) + gelu(at)).astype(BF16)
            h_out[mb, :, cut(j)] = result

            @pl.when(not_last)
            def _(j=j):
                h_piece(mb, j).start()

            pre[1, mb, :, cut(j)] = at
            wide = result.astype(F32)
            squares = squares + row_sum(wide * wide)
        for j in range(CUTS):
            normed[0, mb, :, cut(j)] = (
                h_in[mb, :, cut(j)].astype(F32) * inv * gains_ref[0:1, cut(j)]
            ).astype(BF16)
        for copy in peer_copies(mb):
            copy.start()

        @pl.when(last)
        def _():
            scale = inverse(squares)
            z = (h_out[mb].astype(F32) * scale * out_gain_ref[...]).astype(BF16)
            logits = dot(z, hw[...])
            top = jnp.max(logits, axis=1, keepdims=True)
            exponents = jnp.exp(logits - top)
            denominator = row_sum(exponents)
            target = picked_ids[pl.ds(pl.multiple_of(mb * ROWS, ROWS), ROWS), 0:1]
            one_hot = (target == lax.broadcasted_iota(jnp.int32, logits.shape, 1)).astype(F32)
            picked = row_sum(logits * one_hot)
            dlog[mb] = (exponents / denominator - one_hot).astype(BF16)
            for copy in head_copies(mb):
                copy.start()
            losses = jnp.sum(jnp.log(denominator) + top - picked, axis=0, keepdims=True)
            loss_part[...] += jnp.broadcast_to(losses, loss_part.shape)

        return carry

    def part_copy(lane, target):
        return remote(loss_part, loss_in.at[lane], part_send.at[lane], part_recv.at[lane], (odd, target))

    def loss_back():
        return remote(loss_all, loss_all, loss_send.at[0], loss_recv.at[0], (s - 2, y))

    def loss_peer():
        return remote(loss_all, loss_all, loss_send.at[1], loss_recv.at[1], peer)

    def n_copy(layer, owner, lane):
        src = normed.at[layer, :, :, pl.ds(pl.multiple_of(owner * share, share), share)]
        return remote(src, normed_out.at[y], n_send.at[layer, lane], n_recv.at[lane], (2 * k + layer, owner))

    def n_local(layer):
        src = normed.at[layer, :, :, pl.ds(pl.multiple_of(y * share, share), share)]
        return pltpu.make_async_copy(src, normed_out.at[y], local_sem.at[0])

    def n_wait(lane, owner):
        src = normed.at[0, :, :, pl.ds(0, share)]
        return remote(src, normed_out.at[owner], n_send.at[0, lane], n_recv.at[lane], peer)

    def d_copy(layer, owner, lane, mb):
        return remote(
            dpre.at[layer, mb], dpre_out.at[y, mb], d_send.at[layer, lane], d_recv.at[lane], (2 * k + layer, owner)
        )

    def d_local(layer, mb):
        return pltpu.make_async_copy(dpre.at[layer, mb], dpre_out.at[y, mb], local_sem.at[1])

    def d_wait(lane, owner):
        return remote(dpre.at[0], dpre_out.at[owner], d_send.at[0, lane], d_recv.at[lane], peer)

    lanes = ((1, up), (2, down), (3, far))
    arrivals = ((1, down), (2, up), (3, far))

    @pl.when(forward)
    def _():
        loss_part[...] = jnp.zeros_like(loss_part)
        lax.fori_loop(0, count, forward_one, 0)
        for layer in range(2):
            for lane, owner in lanes:
                n_copy(layer, owner, lane).start()
        n_copy(0, y, 0).start()
        n_local(1).start()

        @pl.when(last)
        def _():
            for lane, owner in lanes:
                part_copy(lane, owner).start()
            for lane, owner in lanes:
                part_copy(lane, owner).wait_recv()
            loss_all[...] = loss_part[...] + loss_in[1] + loss_in[2] + loss_in[3]

        @pl.when(not_last)
        def _():
            loss_back().wait_recv()

        @pl.when(not_first)
        def _():
            loss_back().start()

        loss_peer().start()

    def g_piece(mb, j):
        cols = pl.ds(j * step, step)
        return remote(
            g_out.at[mb, :, cols], g_in.at[mb, :, cols], g_send.at[j], g_recv.at[mb, j], (s - 2, y)
        )

    def prepare(mb):
        for copy in peer_copies(mb):
            copy.wait_recv()
        for layer, rows in ((0, h_in), (1, h_mid)):
            squares = jnp.zeros((ROWS, 1), F32)
            for j in range(CUTS):
                h = rows[mb, :, cut(j)].astype(F32)
                squares = squares + row_sum(h * h)
                slope[layer, :, cut(j)] = gelu_slope(pre[layer, mb, :, cut(j)])
            inv_keep[layer] = jnp.broadcast_to(inverse(squares), inv_keep.shape[1:])

    def backward_one(mb, carry):
        @pl.when(last)
        def _():
            for copy in head_copies(mb):
                copy.wait_recv()
            back = dot(dlog[mb], ht[...]) * out_gain_ref[...]
            h = h_out[mb].astype(F32)
            scale = inverse(row_sum(h * h))
            inner = row_sum(back * h)
            g_in[mb] = (scale * back - h * (scale * scale * scale * (1.0 / width) * inner)).astype(BF16)

        for j in range(CUTS):

            @pl.when(not_last)
            def _(j=j):
                g_piece(mb, j).wait_recv()

            d = (g_in[mb, :, cut(j)].astype(F32) * slope[1, :, cut(j)]).astype(BF16)
            dpre[1, mb, :, cut(j)] = d
            product = dot(d, wt[1, cut(j), :])
            if j == 0:
                acc[...] = product
            else:
                acc[...] += product
        inv = inv_keep[1, :, 0:1]
        inner = jnp.zeros((ROWS, 1), F32)
        for j in range(CUTS):
            inner = inner + row_sum(acc[:, cut(j)] * gains_ref[1:2, cut(j)] * h_mid[mb, :, cut(j)].astype(F32))
        pull = inv * inv * inv * (1.0 / width) * inner
        dots = jnp.zeros((ROWS, 1), F32)
        for j in range(CUTS):
            back = acc[:, cut(j)] * gains_ref[1:2, cut(j)]
            g = (
                g_in[mb, :, cut(j)].astype(F32) + (inv * back - h_mid[mb, :, cut(j)].astype(F32) * pull)
            ).astype(BF16)
            acc[:, cut(j)] = g.astype(F32)
            d = (g.astype(F32) * slope[0, :, cut(j)]).astype(BF16)
            dpre[0, mb, :, cut(j)] = d
            dots = dots + row_sum(d.astype(F32) * pre[0, mb, :, cut(j)])

        @pl.when(not_first)
        def _():
            inv = inv_keep[0, :, 0:1]
            pull = inv * inv * (1.0 / width) * dots
            for j in range(CUTS):
                back = dot(dpre[0, mb], wt[0, :, cut(j)]) * gains_ref[0:1, cut(j)]
                g_out[mb, :, cut(j)] = (
                    acc[:, cut(j)] + (inv * back - h_in[mb, :, cut(j)].astype(F32) * pull)
                ).astype(BF16)
                g_piece(mb, j).start()

        for layer in range(2):
            for lane, owner in lanes:
                d_copy(layer, owner, lane, mb).start()
        d_copy(1, y, 0, mb).start()
        d_local(0, mb).start()

        @pl.when(mb < count - 1)
        def _():
            prepare(mb + 1)

        return carry

    @pl.when(backward)
    def _():
        prepare(0)
        lax.fori_loop(0, count, backward_one, 0)
        loss_peer().wait_recv()

    loss_ref[...] = loss_all[...]
    for lane, owner in arrivals:
        n_wait(lane, owner).wait_recv()
        d_wait(lane, owner).wait_recv()

    def sent(ref, sem):
        pltpu.make_async_copy(ref, ref, sem).wait()

    for lane in (1, 2):
        for part in (0, 1):
            sent(w.at[0, 0:half, :], w_send.at[lane, part])

    @pl.when(forward)
    def _():
        for i in range(4):
            sent(w.at[0, 0:half, :], w_send.at[3, i])
        sent(w.at[0, 0:share, :], w_fwd_send.at[1, 0])
        for layer in range(2):
            for lane in (1, 2, 3):
                sent(w.at[0, 0:share, :], w_fwd_send.at[layer, lane])
                sent(normed.at[0, :, :, 0:share], n_send.at[layer, lane])
        sent(normed.at[0, :, :, 0:share], n_send.at[0, 0])
        n_local(1).wait()
        for copy in [remote(ref, ref, peer_send.at[i], peer_recv.at[i, 0], peer) for i, ref in enumerate([h_in, h_mid, pre.at[0], pre.at[1]])]:
            copy.wait_send()

        @pl.when(not_last)
        def _():
            for j in range(CUTS):
                sent(h_out.at[:, :, cut(j)], h_send.at[j])

        @pl.when(last)
        def _():
            sent(h_out, peer_send.at[4])
            sent(dlog, peer_send.at[5])
            for lane in (1, 2, 3):
                sent(loss_part, part_send.at[lane])

        @pl.when(not_first)
        def _():
            sent(loss_all, loss_send.at[0])

        sent(loss_all, loss_send.at[1])
        d_wait(0, y).wait_recv()

    @pl.when(backward)
    def _():
        sent(w.at[0, 0:share, :], w_fwd_send.at[0, 0])
        for layer in range(2):
            for lane in (1, 2, 3):
                sent(dpre.at[0], d_send.at[layer, lane])
        sent(dpre.at[0], d_send.at[1, 0])
        sent(dpre.at[0], local_sem.at[1])

        @pl.when(not_first)
        def _():
            for j in range(CUTS):
                sent(g_out.at[:, :, cut(j)], g_send.at[j])

        n_wait(0, y).wait_recv()


def shards(
    video_ids,
    action_ids,
    target_ids,
    live_lengths,
    video_table,
    action_table,
    layer_gain,
    layer_weight,
    out_gain,
    head_weight,
    live_rows,
):
    width, vocab = head_weight.shape
    share = width // 4
    count = live_rows // ROWS
    ids = jnp.stack([video_ids, action_ids, target_ids])
    other = lax.ppermute(
        layer_gain, "section", [(i, i ^ 1) for i in range(lax.axis_size("section"))]
    )
    odd = lax.axis_index("section") % 2 == 1
    gains = jnp.where(odd, jnp.concatenate([other, layer_gain]), jnp.concatenate([layer_gain, other]))

    vmem = pl.BlockSpec(memory_space=pltpu.VMEM)
    smem = pl.BlockSpec(memory_space=pltpu.SMEM)
    hbm = pl.BlockSpec(memory_space=pl.ANY)
    dma = pltpu.SemaphoreType.DMA
    rows = lambda kind: pltpu.VMEM((count, ROWS, width), kind)
    pair = lambda kind: pltpu.VMEM((2, count, ROWS, width), kind)
    loss, normed, dpre = pl.pallas_call(
        kernel,
        name="stack",
        out_shape=(
            jax.ShapeDtypeStruct((8, 128), F32),
            jax.ShapeDtypeStruct((4, count, ROWS, share), BF16),
            jax.ShapeDtypeStruct((4, count, ROWS, width), BF16),
        ),
        in_specs=[smem, vmem, vmem, vmem, vmem, hbm, hbm, hbm],
        out_specs=(vmem, hbm, hbm),
        scratch_shapes=[
            pltpu.VMEM((2, width, width), BF16),
            pltpu.VMEM((2, width, width), BF16),
            pltpu.VMEM((width, vocab), BF16),
            pltpu.VMEM((vocab, width), BF16),
            rows(BF16),
            rows(BF16),
            rows(BF16),
            pair(F32),
            pair(BF16),
            pair(BF16),
            rows(BF16),
            rows(BF16),
            pltpu.VMEM((count, ROWS, vocab), BF16),
            pltpu.VMEM((ROWS, width), F32),
            pltpu.VMEM((2, ROWS, width), F32),
            pltpu.VMEM((2, ROWS, 128), F32),
            pltpu.VMEM((live_rows, 128), jnp.int32),
            pltpu.VMEM((8, 128), F32),
            pltpu.VMEM((4, 8, 128), F32),
            pltpu.VMEM((8, 128), F32),
            dma((4, 4)),
            dma((2, 4, 2)),
            dma((2, 4)),
            dma((2, 4)),
            dma((2,)),
            dma((CUTS,)),
            dma((count, CUTS)),
            dma((CUTS,)),
            dma((count, CUTS)),
            dma((6,)),
            dma((6, count)),
            dma((2, 4)),
            dma((4,)),
            dma((2, 4)),
            dma((4,)),
            dma((4,)),
            dma((4,)),
            dma((2,)),
            dma((2,)),
        ],
        compiler_params=pltpu.CompilerParams(
            collective_id=0, has_side_effects=True, vmem_limit_bytes=60 * 1024 * 1024
        ),
        cost_estimate=pl.CostEstimate(flops=10**10, bytes_accessed=2 * 10**7, transcendentals=0),
    )(live_lengths, ids, gains, out_gain[None], action_table, video_table, layer_weight, head_weight)
    grad = lax.dot_general(
        normed.reshape(4 * live_rows, share),
        dpre.reshape(4 * live_rows, width),
        (((0,), (0,)), ((), ())),
        preferred_element_type=F32,
    )
    live_count = (jnp.sum(live_lengths) * lax.axis_size("dp")).astype(F32)
    return (loss[0, 0] / live_count, grad[None])


def solution(mesh, live_rows=160):
    in_specs = (
        P("dp", None),
        P("dp", None),
        P("dp", None),
        P("dp", None),
        P(),
        P(),
        P("section", None),
        P("section", "dp", None),
        P(),
        P(),
    )
    out_specs = (P(), P("section", "dp", None))
    return jax.shard_map(
        functools.partial(shards, live_rows=live_rows),
        mesh=mesh,
        in_specs=in_specs,
        out_specs=out_specs,
        check_vma=False,
    )
```

time: 1720 us -> 286 us (0.17)
  waiting for transfers between devices: 1040 us -> 0.01 us
  starting transfers between devices: 331 us -> 0.09 us
  Pallas kernels: 0 us -> 270 us
  matrix products: 206 us -> 5.79 us
  blocking collectives: 67.8 us -> 0 us
  other arithmetic: 37.6 us -> 4.02 us
  local copies, waits for them, and re-layouts: 19.1 us -> 1.18 us
    ppermute x78 -> x1, waiting for transfers between devices: 950 us -> 0.01 us  [shards(): lax.ppermute(layer_gain, 'section', [(i, i ^ 1) for i in range(lax.axis_s...]
    ppermute x78 -> x1, starting transfers between devices: 331 us -> 0.09 us  [shards(): lax.ppermute(layer_gain, 'section', [(i, i ^ 1) for i in range(lax.axis_s...]
    pallas_call x0 -> x1, Pallas kernels: none -> 270 us  [shards(): pl.pallas_call(kernel, name='stack', out_shape=(jax.ShapeDtypeStruct((8,...]
    dot_general x24 -> x1, matrix products: 206 us -> 5.79 us  [shards(): lax.dot_general(normed.reshape(4 * live_rows, share), dpre.reshape(4 * li...]
    all_gather x1 -> x0, waiting for transfers between devices: 79.1 us -> none  [shards(): weight = lax.all_gather(layer_weight[0], 'dp', axis=0, tiled=True)]
    psum x1 -> x0, blocking collectives: 67.8 us -> none  [shards(): loss_sum, live_count = lax.psum((loss_sum, live_count), ('section', 'dp'))]
    convert_element_type x11 -> x0, other arithmetic: 19.4 us -> none  [the longest x1 9.08 us: shards(): running.astype(jnp.bfloat16)]
  transfers between devices with their start and end apart: 80 -> 1, of which waited for: 80 -> 0; matrix products, arithmetic and copies ran while one was open for 0% -> 1% of each run, Pallas kernels for 0% -> 0%
where the time goes in v1:
time: 286 us; the launch traced here: 284 us
  Pallas kernels  270 us (94%)
  matrix products  5.79 us (2%)
  other arithmetic  4.02 us (1%)
  between operations  3.1 us (1%)
    pallas_call x1, Pallas kernels, shards(): pl.pallas_call(kernel, name='stack', out_shape=(jax.ShapeDtypeStruct((8,...  270 us
    dot_general x1, matrix products, shards(): lax.dot_general(normed.reshape(4 * live_rows, share), dpre.reshape(4 * li...  5.79 us
  transfers between devices with their start and end apart: 1, of which 0 were waited for; matrix products, arithmetic and copies ran while one was open for 1% of the time, Pallas kernels for 0%

profile of v1, /device:TPU:0, one launch (start us, length us, event | category | flops | bytes accessed | tf_op | source)
XLA Modules:
  0.0 283.8 jit_solution(11224542840651187889)
XLA Ops:
  0.6 0.1 collective-permute-start
  0.7 1.3 pad_add_fusion.ids_ref
  2.0 1.3 reduce_sum.9
  4.0 0.0 collective-permute-done
  4.0 1.4 maximum_select_fusion.gains_ref
  5.4 269.6 %stack.17 = (f32[8,128]{1,0:T(8,128)}, bf16[4,10,16,512]{3,2,1,0:T(8,128)(2,1)}, bf16[4,10,16,2048]{3,2,1,0:T(8,128)(2,1)}) custom-call(s32[1,8]{1,0:T(1,128)} %lengths_ref.1, s32[3,8,32]{2,1,0:T(8,128)} %pad_add_fusion.ids_ref, f32[2,2048]{1,0:T(2,128)} %maximum_select_fusion.gains_ref, f32[1,2048]{1,0:T(1,128)} %bitcast.16, bf16[8,2048]{1,0:T(8,128)(2,1)} %actions_ref.1, ...), custom_call_target="tpu_custom_call" | custom-call | flops 10000000000 | bytes 20000000 | tf_op jit(solution)/shard_map/stack/pallas_call | solution.py:595
  275.1 1.2 slice.3
  276.9 5.8 %convolution_bitcast_fusion = f32[1,512,2048]{2,1,0:T(8,128)} fusion(bf16[4,10,16,512]{3,2,1,0:T(8,128)(2,1)} %get-tuple-element.6, bf16[4,10,16,2048]{3,2,1,0:T(8,128)(2,1)} %get-tuple-element.7), kind=kOutput, calls=%fused_computation | convolution fusion | flops 1342177280 | bytes 7471104 | tf_op jit(solution)/shard_map/dot_general | solution.py:651
Async XLA Ops:
  0.6 3.4 %collective-permute-start = (f32[1,2048]{1,0:T(1,128)}, f32[1,2048]{1,0:T(1,128)S(1)}, u32[]{:S(2)}, u32[]{:S(2)}) collective-permute-start(f32[1,2048]{1,0:T(1,128)} %param.16), channel_id=1, source_target_pairs={{0,4},{4,0},{8,12},{12,8},{16,20},{20,16},{24,28},{28,24},{32,36},... | collective-permute-start | bytes 24584 | tf_op jit(solution)/shard_map/ppermute | solution.py:583

commit v2 on v1

--- a/solution.py
+++ b/solution.py
@@ -35,8 +35,10 @@
 
 def kernel(
     lengths_ref,
-    ids_ref,
-    gains_ref,
+    video_ids_ref,
+    action_ids_ref,
+    target_ids_ref,
+    gain_ref,
     out_gain_ref,
     actions_ref,
     video_ref,
@@ -61,6 +63,7 @@
     acc,
     slope,
     inv_keep,
+    gains,
     picked_ids,
     loss_part,
     loss_in,
@@ -84,14 +87,22 @@
     part_recv,
     loss_send,
     loss_recv,
+    gain_send,
+    gain_recv,
 ):
     s = lax.axis_index("section")
     y = lax.axis_index("dp")
     planes = lax.axis_size("section") // 2
     k = s // 2
     core = s % 2
-    forward = core == 1
-    backward = core == 0
+    turning = planes - max(1, planes * 3 // 16)
+    late = k >= turning
+    early = k < turning
+    odd_core = core == 1
+    even_core = core == 0
+    forward = odd_core
+    backward = jnp.logical_or(jnp.logical_and(early, odd_core), jnp.logical_and(late, even_core))
+    back_target = 2 * (k - 1) + jnp.where(k - 1 < turning, 1, 0)
     first = k == 0
     last = k == planes - 1
     not_first = k > 0
@@ -120,10 +131,10 @@
             pl.semaphore_signal(barrier, inc=1, device_id=(2 * k + c, other), device_id_type=MESH)
     pl.semaphore_signal(barrier, inc=1, device_id=peer, device_id_type=MESH)
 
-    sections = 2 * planes
-    for other in ((s + 2) % sections, (s + sections - 2) % sections):
-        pl.semaphore_signal(barrier, inc=1, device_id=(other, y), device_id_type=MESH)
-    pl.semaphore_wait(barrier, 9)
+    for plane in ((k + 1) % planes, (k + planes - 1) % planes):
+        for c in (0, 1):
+            pl.semaphore_signal(barrier, inc=1, device_id=(2 * plane + c, y), device_id_type=MESH)
+    pl.semaphore_wait(barrier, 11)
 
     def rows_of(owner, part=None):
         if part is None:
@@ -162,16 +173,29 @@
         direct(layer, 2, 1).start()
         direct(layer, 1, 1).start()
         direct(layer, 2, 0).start()
-        own_to_peer(layer).start()
-        own_local(layer).start()
-
-    @pl.when(forward)
+        gain_peer(layer).start()
+        gains[layer] = gain_ref[...]
+
+    def gain_peer(layer):
+        return remote(gain_ref, gains.at[layer], gain_send.at[0], gain_recv.at[0], peer)
+
+    @pl.when(odd_core)
     def _():
         start_own(1)
-
-    @pl.when(backward)
+        own_local(1).start()
+
+        @pl.when(late)
+        def _():
+            own_to_peer(1).start()
+
+    @pl.when(even_core)
     def _():
         start_own(0)
+        own_to_peer(0).start()
+
+        @pl.when(late)
+        def _():
+            own_local(0).start()
 
     @pl.when(last)
     def _():
@@ -182,16 +206,16 @@
         pltpu.make_async_copy(video_ref, ht, local_sem.at[1]).start()
 
     total = count * ROWS
-    slots = ids_ref.shape[2]
+    slots = video_ids_ref.shape[1]
     place = lax.broadcasted_iota(jnp.int32, (total, slots), 0)
     lane_of = lax.broadcasted_iota(jnp.int32, (total, slots), 1)
     chosen = [jnp.zeros((total, 1), jnp.int32) for _ in range(3)]
     start = jnp.int32(0)
-    for b in range(ids_ref.shape[1]):
+    for b in range(video_ids_ref.shape[0]):
         length = lengths_ref[0, b]
         hit = jnp.logical_and(place == start + lane_of, lane_of < length)
-        for kind in range(3):
-            line = jnp.broadcast_to(ids_ref[kind, b : b + 1, :], (total, slots))
+        for kind, ids_ref in enumerate((video_ids_ref, action_ids_ref, target_ids_ref)):
+            line = jnp.broadcast_to(ids_ref[b : b + 1, :], (total, slots))
             chosen[kind] = chosen[kind] + row_sum(jnp.where(hit, line, 0))
         start = start + length
     picked_ids[...] = jnp.broadcast_to(chosen[2], picked_ids.shape)
@@ -208,40 +232,57 @@
                 rows = rows + jnp.where(chosen[1] == a, actions_ref[a : a + 1, cols].astype(F32), 0.0)
             h_in[:, :, cols] = rows.astype(BF16).reshape(count, ROWS, step)
 
-    @pl.when(forward)
+    block = min(512, width)
+
+    def turn(layer, owner):
+        def one(i, carry):
+            cols = pl.ds(pl.multiple_of(i * block, block), block)
+            wt[layer, cols, rows_of(owner)] = w[layer, rows_of(owner), cols].T
+            return carry
+
+        lax.fori_loop(0, width // block, one, 0)
+
+    gain_peer(0).wait_recv()
+
+    @pl.when(odd_core)
     def _():
         for layer in range(2):
             direct(layer, 1, 0).wait_recv()
             relay(layer, 0).start()
             direct(layer, 2, 1).wait_recv()
             relay(layer, 1).start()
+        own_local(1).wait()
+        own_to_peer(0).wait_recv()
         for layer in range(2):
             direct(layer, 1, 1).wait_recv()
-            to_peer(layer, 1, down).start()
             direct(layer, 2, 0).wait_recv()
-            to_peer(layer, 2, up).start()
+
+        @pl.when(late)
+        def _():
+            for layer in range(2):
+                to_peer(layer, 1, down).start()
+                to_peer(layer, 2, up).start()
+
+        @pl.when(early)
+        def _():
+            for layer in range(2):
+                for owner in (y, down, up):
+                    turn(layer, owner)
+
         for layer in range(2):
             relay(layer, 0).wait_recv()
             relay(layer, 1).wait_recv()
-            to_peer(layer, 3, far).start()
-        own_local(1).wait()
-        own_to_peer(0).wait_recv()
+
+        @pl.when(late)
+        def _():
+            for layer in range(2):
+                to_peer(layer, 3, far).start()
 
     @pl.when(jnp.logical_and(last, forward))
     def _():
         pltpu.make_async_copy(head_ref, hw, local_sem.at[1]).wait()
 
-    block = min(512, width)
-
-    def turn(layer, owner):
-        def one(i, carry):
-            cols = pl.ds(pl.multiple_of(i * block, block), block)
-            wt[layer, cols, rows_of(owner)] = w[layer, rows_of(owner), cols].T
-            return carry
-
-        lax.fori_loop(0, width // block, one, 0)
-
-    @pl.when(backward)
+    @pl.when(jnp.logical_and(late, even_core))
     def _():
         own_local(0).wait()
         turn(0, y)
@@ -292,7 +333,7 @@
 
             h = h_in[mb, :, cut(j)].astype(F32)
             squares = squares + row_sum(h * h)
-            scaled = (h * gains_ref[0:1, cut(j)]).astype(BF16)
+            scaled = (h * gains[0, :, cut(j)]).astype(BF16)
             product = dot(scaled, w[0, cut(j), :])
             if j == 0:
                 acc[...] = product
@@ -311,7 +352,7 @@
         inv_mid = inverse(squares)
         for j in range(CUTS):
             normed[1, mb, :, cut(j)] = (
-                h_mid[mb, :, cut(j)].astype(F32) * inv_mid * gains_ref[1:2, cut(j)]
+                h_mid[mb, :, cut(j)].astype(F32) * inv_mid * gains[1, :, cut(j)]
             ).astype(BF16)
         squares = jnp.zeros((ROWS, 1), F32)
         for j in range(CUTS):
@@ -328,10 +369,13 @@
             squares = squares + row_sum(wide * wide)
         for j in range(CUTS):
             normed[0, mb, :, cut(j)] = (
-                h_in[mb, :, cut(j)].astype(F32) * inv * gains_ref[0:1, cut(j)]
+                h_in[mb, :, cut(j)].astype(F32) * inv * gains[0, :, cut(j)]
             ).astype(BF16)
-        for copy in peer_copies(mb):
-            copy.start()
+
+        @pl.when(late)
+        def _():
+            for copy in peer_copies(mb):
+                copy.start()
 
         @pl.when(last)
         def _():
@@ -378,6 +422,19 @@
             dpre.at[layer, mb], dpre_out.at[y, mb], d_send.at[layer, lane], d_recv.at[lane], (2 * k + layer, owner)
         )
 
+    def send_dpre(layer, mb):
+        for lane, owner in lanes:
+            d_copy(layer, owner, lane, mb).start()
+        here = early if layer == 1 else late
+
+        @pl.when(here)
+        def _():
+            d_local(layer, mb).start()
+
+        @pl.when(jnp.logical_not(here))
+        def _():
+            d_copy(layer, y, 0, mb).start()
+
     def d_local(layer, mb):
         return pltpu.make_async_copy(dpre.at[layer, mb], dpre_out.at[y, mb], local_sem.at[1])
 
@@ -397,33 +454,23 @@
         n_copy(0, y, 0).start()
         n_local(1).start()
 
-        @pl.when(last)
-        def _():
-            for lane, owner in lanes:
-                part_copy(lane, owner).start()
-            for lane, owner in lanes:
-                part_copy(lane, owner).wait_recv()
-            loss_all[...] = loss_part[...] + loss_in[1] + loss_in[2] + loss_in[3]
-
-        @pl.when(not_last)
-        def _():
-            loss_back().wait_recv()
-
-        @pl.when(not_first)
-        def _():
-            loss_back().start()
-
-        loss_peer().start()
+        @pl.when(early)
+        def _():
+            for layer in range(2):
+                turn(layer, far)
 
     def g_piece(mb, j):
         cols = pl.ds(j * step, step)
         return remote(
-            g_out.at[mb, :, cols], g_in.at[mb, :, cols], g_send.at[j], g_recv.at[mb, j], (s - 2, y)
+            g_out.at[mb, :, cols], g_in.at[mb, :, cols], g_send.at[j], g_recv.at[mb, j], (back_target, y)
         )
 
     def prepare(mb):
-        for copy in peer_copies(mb):
-            copy.wait_recv()
+        @pl.when(late)
+        def _():
+            for copy in peer_copies(mb):
+                copy.wait_recv()
+
         for layer, rows in ((0, h_in), (1, h_mid)):
             squares = jnp.zeros((ROWS, 1), F32)
             for j in range(CUTS):
@@ -459,11 +506,11 @@
         inv = inv_keep[1, :, 0:1]
         inner = jnp.zeros((ROWS, 1), F32)
         for j in range(CUTS):
-            inner = inner + row_sum(acc[:, cut(j)] * gains_ref[1:2, cut(j)] * h_mid[mb, :, cut(j)].astype(F32))
+            inner = inner + row_sum(acc[:, cut(j)] * gains[1, :, cut(j)] * h_mid[mb, :, cut(j)].astype(F32))
         pull = inv * inv * inv * (1.0 / width) * inner
         dots = jnp.zeros((ROWS, 1), F32)
         for j in range(CUTS):
-            back = acc[:, cut(j)] * gains_ref[1:2, cut(j)]
+            back = acc[:, cut(j)] * gains[1, :, cut(j)]
             g = (
                 g_in[mb, :, cut(j)].astype(F32) + (inv * back - h_mid[mb, :, cut(j)].astype(F32) * pull)
             ).astype(BF16)
@@ -477,17 +524,14 @@
             inv = inv_keep[0, :, 0:1]
             pull = inv * inv * (1.0 / width) * dots
             for j in range(CUTS):
-                back = dot(dpre[0, mb], wt[0, :, cut(j)]) * gains_ref[0:1, cut(j)]
+                back = dot(dpre[0, mb], wt[0, :, cut(j)]) * gains[0, :, cut(j)]
                 g_out[mb, :, cut(j)] = (
                     acc[:, cut(j)] + (inv * back - h_in[mb, :, cut(j)].astype(F32) * pull)
                 ).astype(BF16)
                 g_piece(mb, j).start()
 
-        for layer in range(2):
-            for lane, owner in lanes:
-                d_copy(layer, owner, lane, mb).start()
-        d_copy(1, y, 0, mb).start()
-        d_local(0, mb).start()
+        send_dpre(0, mb)
+        send_dpre(1, mb)
 
         @pl.when(mb < count - 1)
         def _():
@@ -499,9 +543,33 @@
     def _():
         prepare(0)
         lax.fori_loop(0, count, backward_one, 0)
+
+    @pl.when(odd_core)
+    def _():
+        @pl.when(last)
+        def _():
+            for lane, owner in lanes:
+                part_copy(lane, owner).start()
+            for lane, owner in lanes:
+                part_copy(lane, owner).wait_recv()
+            loss_all[...] = loss_part[...] + loss_in[1] + loss_in[2] + loss_in[3]
+
+        @pl.when(not_last)
+        def _():
+            loss_back().wait_recv()
+
+        @pl.when(not_first)
+        def _():
+            loss_back().start()
+
+        loss_peer().start()
+
+    @pl.when(even_core)
+    def _():
         loss_peer().wait_recv()
 
-    loss_ref[...] = loss_all[...]
+    live_count = (start * lax.axis_size("dp")).astype(F32)
+    loss_ref[0, 0] = loss_all[0, 0] / live_count
     for lane, owner in arrivals:
         n_wait(lane, owner).wait_recv()
         d_wait(lane, owner).wait_recv()
@@ -509,23 +577,30 @@
     def sent(ref, sem):
         pltpu.make_async_copy(ref, ref, sem).wait()
 
+    sent(gain_ref, gain_send.at[0])
     for lane in (1, 2):
         for part in (0, 1):
             sent(w.at[0, 0:half, :], w_send.at[lane, part])
 
-    @pl.when(forward)
+    @pl.when(odd_core)
     def _():
         for i in range(4):
             sent(w.at[0, 0:half, :], w_send.at[3, i])
-        sent(w.at[0, 0:share, :], w_fwd_send.at[1, 0])
         for layer in range(2):
             for lane in (1, 2, 3):
-                sent(w.at[0, 0:share, :], w_fwd_send.at[layer, lane])
                 sent(normed.at[0, :, :, 0:share], n_send.at[layer, lane])
         sent(normed.at[0, :, :, 0:share], n_send.at[0, 0])
         n_local(1).wait()
-        for copy in [remote(ref, ref, peer_send.at[i], peer_recv.at[i, 0], peer) for i, ref in enumerate([h_in, h_mid, pre.at[0], pre.at[1]])]:
-            copy.wait_send()
+
+        @pl.when(late)
+        def _():
+            sent(w.at[0, 0:share, :], w_fwd_send.at[1, 0])
+            for layer in range(2):
+                for lane in (1, 2, 3):
+                    sent(w.at[0, 0:share, :], w_fwd_send.at[layer, lane])
+            for i, ref in enumerate([h_in, h_mid, pre.at[0], pre.at[1]]):
+                sent(ref, peer_send.at[i])
+            d_wait(0, y).wait_recv()
 
         @pl.when(not_last)
         def _():
@@ -544,23 +619,65 @@
             sent(loss_all, loss_send.at[0])
 
         sent(loss_all, loss_send.at[1])
-        d_wait(0, y).wait_recv()
+
+    @pl.when(even_core)
+    def _():
+        sent(w.at[0, 0:share, :], w_fwd_send.at[0, 0])
+        n_wait(0, y).wait_recv()
+
+        @pl.when(early)
+        def _():
+            d_wait(0, y).wait_recv()
 
     @pl.when(backward)
     def _():
-        sent(w.at[0, 0:share, :], w_fwd_send.at[0, 0])
         for layer in range(2):
             for lane in (1, 2, 3):
                 sent(dpre.at[0], d_send.at[layer, lane])
-        sent(dpre.at[0], d_send.at[1, 0])
         sent(dpre.at[0], local_sem.at[1])
+
+        @pl.when(early)
+        def _():
+            sent(dpre.at[0], d_send.at[0, 0])
+
+        @pl.when(late)
+        def _():
+            sent(dpre.at[0], d_send.at[1, 0])
 
         @pl.when(not_first)
         def _():
             for j in range(CUTS):
                 sent(g_out.at[:, :, cut(j)], g_send.at[j])
 
-        n_wait(0, y).wait_recv()
+
+def product_kernel(normed_ref, dpre_ref, out_ref, turned):
+    @pl.when(pl.program_id(0) == 0)
+    def _():
+        turned[...] = normed_ref[...].T
+
+    out_ref[0] = dot(turned[...], dpre_ref[...])
+
+
+def product(normed, dpre):
+    rows, share = normed.shape
+    width = dpre.shape[1]
+    step = min(512, width)
+    return pl.pallas_call(
+        product_kernel,
+        name="weight_grad",
+        grid=(width // step,),
+        out_shape=jax.ShapeDtypeStruct((1, share, width), F32),
+        in_specs=[
+            pl.BlockSpec((rows, share), lambda i: (0, 0)),
+            pl.BlockSpec((rows, step), lambda i: (0, i)),
+        ],
+        out_specs=pl.BlockSpec((1, share, step), lambda i: (0, 0, i)),
+        scratch_shapes=[pltpu.VMEM((share, rows), BF16)],
+        compiler_params=pltpu.CompilerParams(vmem_limit_bytes=32 * 1024 * 1024),
+        cost_estimate=pl.CostEstimate(
+            flops=2 * rows * share * width, bytes_accessed=6 * share * width, transcendentals=0
+        ),
+    )(normed, dpre)
 
 
 def shards(
@@ -579,12 +696,6 @@
     width, vocab = head_weight.shape
     share = width // 4
     count = live_rows // ROWS
-    ids = jnp.stack([video_ids, action_ids, target_ids])
-    other = lax.ppermute(
-        layer_gain, "section", [(i, i ^ 1) for i in range(lax.axis_size("section"))]
-    )
-    odd = lax.axis_index("section") % 2 == 1
-    gains = jnp.where(odd, jnp.concatenate([other, layer_gain]), jnp.concatenate([layer_gain, other]))
 
     vmem = pl.BlockSpec(memory_space=pltpu.VMEM)
     smem = pl.BlockSpec(memory_space=pltpu.SMEM)
@@ -596,12 +707,12 @@
         kernel,
         name="stack",
         out_shape=(
-            jax.ShapeDtypeStruct((8, 128), F32),
+            jax.ShapeDtypeStruct((1, 1), F32),
             jax.ShapeDtypeStruct((4, count, ROWS, share), BF16),
             jax.ShapeDtypeStruct((4, count, ROWS, width), BF16),
         ),
-        in_specs=[smem, vmem, vmem, vmem, vmem, hbm, hbm, hbm],
-        out_specs=(vmem, hbm, hbm),
+        in_specs=[smem, vmem, vmem, vmem, vmem, vmem, vmem, hbm, hbm, hbm],
+        out_specs=(smem, hbm, hbm),
         scratch_shapes=[
             pltpu.VMEM((2, width, width), BF16),
             pltpu.VMEM((2, width, width), BF16),
@@ -619,6 +730,7 @@
             pltpu.VMEM((ROWS, width), F32),
             pltpu.VMEM((2, ROWS, width), F32),
             pltpu.VMEM((2, ROWS, 128), F32),
+            pltpu.VMEM((2, 1, width), F32),
             pltpu.VMEM((live_rows, 128), jnp.int32),
             pltpu.VMEM((8, 128), F32),
             pltpu.VMEM((4, 8, 128), F32),
@@ -642,20 +754,27 @@
             dma((4,)),
             dma((2,)),
             dma((2,)),
+            dma((1,)),
+            dma((1,)),
         ],
         compiler_params=pltpu.CompilerParams(
             collective_id=0, has_side_effects=True, vmem_limit_bytes=60 * 1024 * 1024
         ),
         cost_estimate=pl.CostEstimate(flops=10**10, bytes_accessed=2 * 10**7, transcendentals=0),
-    )(live_lengths, ids, gains, out_gain[None], action_table, video_table, layer_weight, head_weight)
-    grad = lax.dot_general(
-        normed.reshape(4 * live_rows, share),
-        dpre.reshape(4 * live_rows, width),
-        (((0,), (0,)), ((), ())),
-        preferred_element_type=F32,
+    )(
+        live_lengths,
+        video_ids,
+        action_ids,
+        target_ids,
+        layer_gain,
+        out_gain[None],
+        action_table,
+        video_table,
+        layer_weight,
+        head_weight,
     )
-    live_count = (jnp.sum(live_lengths) * lax.axis_size("dp")).astype(F32)
-    return (loss[0, 0] / live_count, grad[None])
+    grad = product(normed.reshape(4 * live_rows, share), dpre.reshape(4 * live_rows, width))
+    return (loss[0, 0], grad)
 
 
 def solution(mesh, live_rows=160):

time: 286 us -> 273 us (0.955)
  matrix products: 5.79 us -> 0 us
  Pallas kernels: 270 us -> 265 us
  other arithmetic: 4.02 us -> 0 us
    dot_general x1 -> x0, matrix products: 5.79 us -> none  [shards(): lax.dot_general(normed.reshape(4 * live_rows, share), dpre.reshape(4 * li...]
    pallas_call x1 -> x2, Pallas kernels: 270 us -> 265 us  [the longest x1 261 us: shards(): pl.pallas_call(kernel, name='stack', out_shape=(jax.ShapeDtypeStruct((1,...]
  transfers between devices with their start and end apart: 1 -> 0, of which waited for: 0 -> 0; matrix products, arithmetic and copies ran while one was open for 1% -> 0% of each run, Pallas kernels for 0% -> 0%
where the time goes in v2:
time: 273 us; the launch traced here: 270 us
  Pallas kernels  265 us (97%)
  local copies, waits for them, and re-layouts  2.82 us (1%)
    pallas_call x1, Pallas kernels, shards(): pl.pallas_call(kernel, name='stack', out_shape=(jax.ShapeDtypeStruct((1,...  261 us

profile of v2, /device:TPU:0, one launch (start us, length us, event | category | flops | bytes accessed | tf_op | source)
XLA Modules:
  0.0 270.3 jit_solution(7439895767355420388)
XLA Ops:
  0.6 261.1 %stack.1 = (f32[1,1]{1,0:T(1,128)}, bf16[4,10,16,512]{3,2,1,0:T(8,128)(2,1)}, bf16[4,10,16,2048]{3,2,1,0:T(8,128)(2,1)}) custom-call(s32[1,8]{1,0:T(1,128)} %lengths_ref.1, s32[8,32]{1,0:T(8,128)} %video_ids_ref.1, s32[8,32]{1,0:T(8,128)} %action_ids_ref.1, s32[8,32]{1,0:T(8,128)} %target_ids_ref.1, f32[1,2048]{1,0:T(1,128)} %gain_ref.1, f32[1,2048]{1,0:T(1,128)} %bitcast.6, ...), custom_call_target="tpu_custom_call" | custom-call | flops 10000000000 | bytes 20000000 | tf_op jit(solution)/shard_map/stack/pallas_call | solution.py:706
  261.7 0.0 copy-start
  261.7 1.7 copy-done
  263.4 0.0 copy-start.1
  263.4 1.1 copy-done.1
  264.5 4.1 %weight_grad.1 = f32[1,512,2048]{2,1,0:T(8,128)} custom-call(bf16[640,512]{1,0:T(8,128)(2,1)S(1)} %bitcast.5, bf16[640,2048]{1,0:T(8,128)(2,1)S(1)} %bitcast.4), custom_call_target="tpu_custom_call" | custom-call | flops 1342177280 | bytes 6291456 | tf_op jit(solution)/shard_map/weight_grad/pallas_call | solution.py:665
Async XLA Ops:
  261.7 1.7 copy-start
  263.4 1.1 copy-start.1

commit v3 on v2

--- a/solution.py
+++ b/solution.py
@@ -61,6 +61,7 @@
     g_out,
     dlog,
     acc,
+    raw,
     slope,
     inv_keep,
     gains,
@@ -89,6 +90,12 @@
     loss_recv,
     gain_send,
     gain_recv,
+    held,
+    held_send,
+    held_recv,
+    back_send,
+    back_recv,
+    go_sem,
 ):
     s = lax.axis_index("section")
     y = lax.axis_index("dp")
@@ -110,7 +117,8 @@
 
     width = w.shape[2]
     share = width // 4
-    half = share // 2
+    halves = (share * 3 // 8, share // 8)
+    main = 2 * halves[0]
     step = width // CUTS
     count = h_in.shape[0]
     vocab = hw.shape[1]
@@ -134,27 +142,83 @@
     for plane in ((k + 1) % planes, (k + planes - 1) % planes):
         for c in (0, 1):
             pl.semaphore_signal(barrier, inc=1, device_id=(2 * plane + c, y), device_id_type=MESH)
-    pl.semaphore_wait(barrier, 11)
-
-    def rows_of(owner, part=None):
-        if part is None:
-            return pl.ds(pl.multiple_of(owner * share, share), share)
-        return pl.ds(pl.multiple_of(owner * share + part * half, half), half)
-
-    def direct(layer, lane, part):
-        target = up if lane == 1 else down
+
+    group = planes // 4
+    helped = k < group
+    helper = k >= planes - group
+    friend = jnp.where(helped, k + planes - group, k - planes + group)
+
+    @pl.when(jnp.logical_or(helped, helper))
+    def _():
+        for c in (0, 1):
+            pl.semaphore_signal(barrier, inc=1, device_id=(2 * friend + c, y), device_id_type=MESH)
+
+    pl.semaphore_wait(barrier, 11 + jnp.where(jnp.logical_or(helped, helper), 2, 0))
+
+    def rows_of(owner):
+        return pl.ds(pl.multiple_of(owner * share, share), share)
+
+    def piece(kind, part):
+        return kind * main + part * halves[kind], halves[kind]
+
+    def piece_of(owner, kind, part):
+        offset, size = piece(kind, part)
+        return pl.ds(pl.multiple_of(owner * share + offset, 16), size)
+
+    def direct(layer, lane, kind, part):
+        offset, size = piece(kind, part)
         return remote(
-            weight_ref.at[0, part * half : (part + 1) * half, :],
-            w.at[layer, rows_of(y, part), :],
-            w_send.at[lane, part],
-            w_recv.at[layer, lane, part],
-            (odd, target),
+            weight_ref.at[0, offset : offset + size, :],
+            w.at[layer, piece_of(y, kind, part), :],
+            w_send.at[lane, 2 * kind + part],
+            w_recv.at[layer, lane, 2 * kind + part],
+            (odd, up if lane == 1 else down),
         )
 
-    def relay(layer, part):
+    def relay(layer, kind, part):
         owner, target = (down, up) if part == 0 else (up, down)
-        block = w.at[layer, rows_of(owner, part), :]
-        return remote(block, block, w_send.at[3, 2 * layer + part], w_recv.at[layer, 3, part], (odd, target))
+        block = w.at[layer, piece_of(owner, kind, part), :]
+        return remote(
+            block, block, w_send.at[3 + layer, 2 * kind + part], w_recv.at[layer, 3, 2 * kind + part], (odd, target)
+        )
+
+    friend_odd = 2 * friend + 1
+
+    def to_helper(layer, part):
+        offset, size = piece(1, part)
+        return remote(
+            weight_ref.at[0, offset : offset + size, :],
+            held.at[layer, y, part],
+            held_send.at[0, part],
+            held_recv.at[layer, 0, part],
+            (friend_odd, y),
+        )
+
+    def held_direct(layer, lane, part):
+        block = held.at[layer, y, part]
+        return remote(
+            block,
+            block,
+            held_send.at[1 + 2 * layer + (lane - 1), part],
+            held_recv.at[layer, lane, part],
+            (odd, up if lane == 1 else down),
+        )
+
+    def held_relay(layer, part):
+        owner, target = (down, up) if part == 0 else (up, down)
+        block = held.at[layer, owner, part]
+        return remote(block, block, held_send.at[5 + layer, part], held_recv.at[layer, 3, part], (odd, target))
+
+    owners = {1: down, 2: up, 3: far}
+
+    def hand_back(layer, lane, part):
+        return remote(
+            held.at[layer, owners[lane], part],
+            w.at[layer, piece_of(owners[lane], 1, part), :],
+            back_send.at[layer, lane, part],
+            back_recv.at[layer, lane, part],
+            (friend_odd, y),
+        )
 
     def to_peer(layer, lane, owner):
         block = w.at[layer, rows_of(owner), :]
@@ -169,18 +233,58 @@
         return pltpu.make_async_copy(weight_ref.at[0], w.at[layer, rows_of(y), :], local_sem.at[0])
 
     def start_own(layer):
-        direct(layer, 1, 0).start()
-        direct(layer, 2, 1).start()
-        direct(layer, 1, 1).start()
-        direct(layer, 2, 0).start()
+        @pl.when(helped)
+        def _():
+            to_helper(layer, 0).start()
+            to_helper(layer, 1).start()
+
+        for kind in (0, 1):
+
+            def one_kind(kind=kind):
+                direct(layer, 1, kind, 0).start()
+                direct(layer, 2, kind, 1).start()
+                direct(layer, 1, kind, 1).start()
+                direct(layer, 2, kind, 0).start()
+
+            if kind == 0:
+                one_kind()
+            else:
+                pl.when(jnp.logical_not(helped))(one_kind)
+
+    def gain_peer(layer):
+        return remote(gain_ref, gains.at[layer], gain_send.at[0], gain_recv.at[0], peer)
+
+    def exchange_gain(layer):
         gain_peer(layer).start()
         gains[layer] = gain_ref[...]
 
-    def gain_peer(layer):
-        return remote(gain_ref, gains.at[layer], gain_send.at[0], gain_recv.at[0], peer)
-
     @pl.when(odd_core)
     def _():
+        exchange_gain(1)
+
+        @pl.when(helper)
+        def _():
+            for part in (0, 1):
+                for layer in (0, 1):
+                    to_helper(layer, part).wait_recv()
+                    held_direct(layer, 1 + part, part).start()
+                    held_direct(layer, 2 - part, part).start()
+            pl.semaphore_signal(go_sem, inc=1, device_id=peer, device_id_type=MESH)
+
+        @pl.when(helper)
+        def _():
+            for part in (0, 1):
+                for layer in (0, 1):
+                    held_direct(layer, 1 + part, part).wait_recv()
+                    held_relay(layer, part).start()
+                    hand_back(layer, 1 + part, part).start()
+                    held_direct(layer, 2 - part, part).wait_recv()
+                    hand_back(layer, 2 - part, part).start()
+            for part in (0, 1):
+                for layer in (0, 1):
+                    held_relay(layer, part).wait_recv()
+                    hand_back(layer, 3, part).start()
+
         start_own(1)
         own_local(1).start()
 
@@ -190,8 +294,14 @@
 
     @pl.when(even_core)
     def _():
+        exchange_gain(0)
+        own_to_peer(0).start()
+
+        @pl.when(helper)
+        def _():
+            pl.semaphore_wait(go_sem, 1)
+
         start_own(0)
-        own_to_peer(0).start()
 
         @pl.when(late)
         def _():
@@ -244,39 +354,63 @@
 
     gain_peer(0).wait_recv()
 
+    def ring(kind):
+        for layer in range(2):
+            direct(layer, 1, kind, 0).wait_recv()
+            relay(layer, kind, 0).start()
+            direct(layer, 2, kind, 1).wait_recv()
+            relay(layer, kind, 1).start()
+
+    def ring_rest(kind):
+        for layer in range(2):
+            direct(layer, 1, kind, 1).wait_recv()
+            direct(layer, 2, kind, 0).wait_recv()
+
+    def ring_far(kind):
+        for layer in range(2):
+            relay(layer, kind, 0).wait_recv()
+            relay(layer, kind, 1).wait_recv()
+
     @pl.when(odd_core)
     def _():
-        for layer in range(2):
-            direct(layer, 1, 0).wait_recv()
-            relay(layer, 0).start()
-            direct(layer, 2, 1).wait_recv()
-            relay(layer, 1).start()
+        ring(0)
         own_local(1).wait()
         own_to_peer(0).wait_recv()
-        for layer in range(2):
-            direct(layer, 1, 1).wait_recv()
-            direct(layer, 2, 0).wait_recv()
-
-        @pl.when(late)
-        def _():
+
+        @pl.when(helped)
+        def _():
+            ring_rest(0)
+            ring_far(0)
             for layer in range(2):
-                to_peer(layer, 1, down).start()
-                to_peer(layer, 2, up).start()
-
-        @pl.when(early)
-        def _():
-            for layer in range(2):
-                for owner in (y, down, up):
-                    turn(layer, owner)
-
-        for layer in range(2):
-            relay(layer, 0).wait_recv()
-            relay(layer, 1).wait_recv()
-
-        @pl.when(late)
-        def _():
-            for layer in range(2):
-                to_peer(layer, 3, far).start()
+                for lane in (1, 2, 3):
+                    for part in (0, 1):
+                        hand_back(layer, lane, part).wait_recv()
+
+        @pl.when(jnp.logical_not(helped))
+        def _():
+            ring(1)
+            ring_rest(0)
+            ring_rest(1)
+
+            @pl.when(late)
+            def _():
+                for layer in range(2):
+                    to_peer(layer, 1, down).start()
+                    to_peer(layer, 2, up).start()
+
+            @pl.when(early)
+            def _():
+                for layer in range(2):
+                    for owner in (y, down, up):
+                        turn(layer, owner)
+
+            ring_far(0)
+            ring_far(1)
+
+            @pl.when(late)
+            def _():
+                for layer in range(2):
+                    to_peer(layer, 3, far).start()
 
     @pl.when(jnp.logical_and(last, forward))
     def _():
@@ -299,6 +433,59 @@
         for i in range(CUTS):
             ht[:, i * step : (i + 1) * step] = hw[i * step : (i + 1) * step, :].T
 
+    def sent(ref, sem):
+        pltpu.make_async_copy(ref, ref, sem).wait()
+
+    def gather_sent():
+        sent(gain_ref, gain_send.at[0])
+
+        def parts_sent(send, kind):
+            for part in (0, 1):
+                sent(w.at[0, 0 : halves[kind], :], send.at[2 * kind + part])
+
+        for lane in (1, 2):
+            parts_sent(w_send.at[lane], 0)
+
+        @pl.when(jnp.logical_not(helped))
+        def _():
+            for lane in (1, 2):
+                parts_sent(w_send.at[lane], 1)
+
+        @pl.when(helped)
+        def _():
+            for part in (0, 1):
+                sent(held.at[0, 0, 0], held_send.at[0, part])
+
+        @pl.when(odd_core)
+        def _():
+            for layer in (0, 1):
+                parts_sent(w_send.at[3 + layer], 0)
+
+            @pl.when(jnp.logical_not(helped))
+            def _():
+                for layer in (0, 1):
+                    parts_sent(w_send.at[3 + layer], 1)
+
+            @pl.when(helper)
+            def _():
+                for part in (0, 1):
+                    for i in range(1, 7):
+                        sent(held.at[0, 0, 0], held_send.at[i, part])
+                    for layer in (0, 1):
+                        for lane in (1, 2, 3):
+                            sent(held.at[0, 0, 0], back_send.at[layer, lane, part])
+
+            @pl.when(late)
+            def _():
+                sent(w.at[0, 0:share, :], w_fwd_send.at[1, 0])
+                for layer in range(2):
+                    for lane in (1, 2, 3):
+                        sent(w.at[0, 0:share, :], w_fwd_send.at[layer, lane])
+
+        @pl.when(even_core)
+        def _():
+            sent(w.at[0, 0:share, :], w_fwd_send.at[0, 0])
+
     def h_piece(mb, j):
         cols = pl.ds(j * step, step)
         return remote(
@@ -323,24 +510,24 @@
     def cut(j):
         return slice(j * step, (j + 1) * step)
 
-    def forward_one(mb, carry):
-        squares = jnp.zeros((ROWS, 1), F32)
+    def fold(x):
+        return sum(x[:, i : i + 128] for i in range(0, x.shape[1], 128))
+
+    def forward_one(mb, carry, is_first, is_last):
+        squares = jnp.zeros((ROWS, 128), F32)
         for j in range(CUTS):
-
-            @pl.when(not_first)
-            def _(j=j):
+            if not is_first:
                 h_piece(mb, j).wait_recv()
-
             h = h_in[mb, :, cut(j)].astype(F32)
-            squares = squares + row_sum(h * h)
-            scaled = (h * gains[0, :, cut(j)]).astype(BF16)
-            product = dot(scaled, w[0, cut(j), :])
+            squares = squares + fold(h * h)
+            product = dot((h * gains[0, :, cut(j)]).astype(BF16), w[0, cut(j), :])
             if j == 0:
                 acc[...] = product
             else:
                 acc[...] += product
-        inv = inverse(squares)
-        squares = jnp.zeros((ROWS, 1), F32)
+        inv = inverse(row_sum(squares))
+        squares = jnp.zeros((ROWS, 128), F32)
+        opening = None
         for j in range(CUTS):
             h = h_in[mb, :, cut(j)].astype(F32)
             at = acc[:, cut(j)] * inv
@@ -348,38 +535,37 @@
             result = (h + gelu(at)).astype(BF16)
             h_mid[mb, :, cut(j)] = result
             wide = result.astype(F32)
-            squares = squares + row_sum(wide * wide)
-        inv_mid = inverse(squares)
+            squares = squares + fold(wide * wide)
+            scaled = (wide * gains[1, :, cut(j)]).astype(BF16)
+            raw[:, cut(j)] = scaled
+            part = dot(scaled, w[1, cut(j), cut(0)])
+            opening = part if opening is None else opening + part
+        inv_mid = inverse(row_sum(squares))
+        squares = jnp.zeros((ROWS, 128), F32)
         for j in range(CUTS):
-            normed[1, mb, :, cut(j)] = (
-                h_mid[mb, :, cut(j)].astype(F32) * inv_mid * gains[1, :, cut(j)]
-            ).astype(BF16)
-        squares = jnp.zeros((ROWS, 1), F32)
-        for j in range(CUTS):
-            at = dot(normed[1, mb], w[1, :, cut(j)])
+            at = (opening if j == 0 else dot(raw[...], w[1, :, cut(j)])) * inv_mid
             result = (h_mid[mb, :, cut(j)].astype(F32) + gelu(at)).astype(BF16)
             h_out[mb, :, cut(j)] = result
-
-            @pl.when(not_last)
-            def _(j=j):
+            if not is_last:
                 h_piece(mb, j).start()
-
             pre[1, mb, :, cut(j)] = at
             wide = result.astype(F32)
-            squares = squares + row_sum(wide * wide)
+            squares = squares + fold(wide * wide)
         for j in range(CUTS):
             normed[0, mb, :, cut(j)] = (
                 h_in[mb, :, cut(j)].astype(F32) * inv * gains[0, :, cut(j)]
             ).astype(BF16)
+            normed[1, mb, :, cut(j)] = (
+                h_mid[mb, :, cut(j)].astype(F32) * inv_mid * gains[1, :, cut(j)]
+            ).astype(BF16)
 
         @pl.when(late)
         def _():
             for copy in peer_copies(mb):
                 copy.start()
 
-        @pl.when(last)
-        def _():
-            scale = inverse(squares)
+        if is_last:
+            scale = inverse(row_sum(squares))
             z = (h_out[mb].astype(F32) * scale * out_gain_ref[...]).astype(BF16)
             logits = dot(z, hw[...])
             top = jnp.max(logits, axis=1, keepdims=True)
@@ -447,7 +633,19 @@
     @pl.when(forward)
     def _():
         loss_part[...] = jnp.zeros_like(loss_part)
-        lax.fori_loop(0, count, forward_one, 0)
+
+        @pl.when(first)
+        def _():
+            lax.fori_loop(0, count, functools.partial(forward_one, is_first=True, is_last=False), 0)
+
+        @pl.when(jnp.logical_and(not_first, not_last))
+        def _():
+            lax.fori_loop(0, count, functools.partial(forward_one, is_first=False, is_last=False), 0)
+
+        @pl.when(last)
+        def _():
+            lax.fori_loop(0, count, functools.partial(forward_one, is_first=False, is_last=True), 0)
+
         for layer in range(2):
             for lane, owner in lanes:
                 n_copy(layer, owner, lane).start()
@@ -458,6 +656,12 @@
         def _():
             for layer in range(2):
                 turn(layer, far)
+
+        @pl.when(helped)
+        def _():
+            for layer in range(2):
+                for owner in (y, down, up):
+                    turn(layer, owner)
 
     def g_piece(mb, j):
         cols = pl.ds(j * step, step)
@@ -479,9 +683,8 @@
                 slope[layer, :, cut(j)] = gelu_slope(pre[layer, mb, :, cut(j)])
             inv_keep[layer] = jnp.broadcast_to(inverse(squares), inv_keep.shape[1:])
 
-    def backward_one(mb, carry):
-        @pl.when(last)
-        def _():
+    def backward_one(mb, carry, is_first, is_last):
+        if is_last:
             for copy in head_copies(mb):
                 copy.wait_recv()
             back = dot(dlog[mb], ht[...]) * out_gain_ref[...]
@@ -490,48 +693,49 @@
             inner = row_sum(back * h)
             g_in[mb] = (scale * back - h * (scale * scale * scale * (1.0 / width) * inner)).astype(BF16)
 
+        dots = jnp.zeros((ROWS, 128), F32)
         for j in range(CUTS):
-
-            @pl.when(not_last)
-            def _(j=j):
+            if not is_last:
                 g_piece(mb, j).wait_recv()
-
             d = (g_in[mb, :, cut(j)].astype(F32) * slope[1, :, cut(j)]).astype(BF16)
             dpre[1, mb, :, cut(j)] = d
+            dots = dots + fold(d.astype(F32) * pre[1, mb, :, cut(j)])
             product = dot(d, wt[1, cut(j), :])
             if j == 0:
                 acc[...] = product
             else:
                 acc[...] += product
+        if is_first:
+            send_dpre(1, mb)
         inv = inv_keep[1, :, 0:1]
-        inner = jnp.zeros((ROWS, 1), F32)
-        for j in range(CUTS):
-            inner = inner + row_sum(acc[:, cut(j)] * gains[1, :, cut(j)] * h_mid[mb, :, cut(j)].astype(F32))
-        pull = inv * inv * inv * (1.0 / width) * inner
-        dots = jnp.zeros((ROWS, 1), F32)
+        pull = inv * inv * (1.0 / width) * row_sum(dots)
+        dots = jnp.zeros((ROWS, 128), F32)
+        opening = None
         for j in range(CUTS):
             back = acc[:, cut(j)] * gains[1, :, cut(j)]
             g = (
                 g_in[mb, :, cut(j)].astype(F32) + (inv * back - h_mid[mb, :, cut(j)].astype(F32) * pull)
-            ).astype(BF16)
-            acc[:, cut(j)] = g.astype(F32)
-            d = (g.astype(F32) * slope[0, :, cut(j)]).astype(BF16)
+            ).astype(BF16).astype(F32)
+            d = (g * slope[0, :, cut(j)]).astype(BF16)
             dpre[0, mb, :, cut(j)] = d
-            dots = dots + row_sum(d.astype(F32) * pre[0, mb, :, cut(j)])
-
-        @pl.when(not_first)
-        def _():
+            if not is_first:
+                acc[:, cut(j)] = g
+                dots = dots + fold(d.astype(F32) * pre[0, mb, :, cut(j)])
+                part = dot(d, wt[0, cut(j), cut(0)])
+                opening = part if opening is None else opening + part
+        if not is_first:
             inv = inv_keep[0, :, 0:1]
-            pull = inv * inv * (1.0 / width) * dots
+            pull = inv * inv * (1.0 / width) * row_sum(dots)
             for j in range(CUTS):
-                back = dot(dpre[0, mb], wt[0, :, cut(j)]) * gains[0, :, cut(j)]
+                back = (opening if j == 0 else dot(dpre[0, mb], wt[0, :, cut(j)])) * gains[0, :, cut(j)]
                 g_out[mb, :, cut(j)] = (
                     acc[:, cut(j)] + (inv * back - h_in[mb, :, cut(j)].astype(F32) * pull)
                 ).astype(BF16)
                 g_piece(mb, j).start()
 
         send_dpre(0, mb)
-        send_dpre(1, mb)
+        if not is_first:
+            send_dpre(1, mb)
 
         @pl.when(mb < count - 1)
         def _():
@@ -542,7 +746,19 @@
     @pl.when(backward)
     def _():
         prepare(0)
-        lax.fori_loop(0, count, backward_one, 0)
+
+        @pl.when(first)
+        def _():
+            lax.fori_loop(0, count, functools.partial(backward_one, is_first=True, is_last=False), 0)
+
+        @pl.when(jnp.logical_and(not_first, not_last))
+        def _():
+            lax.fori_loop(0, count, functools.partial(backward_one, is_first=False, is_last=False), 0)
+
+        @pl.when(last)
+        def _():
+            lax.fori_loop(0, count, functools.partial(backward_one, is_first=False, is_last=True), 0)
+
 
     @pl.when(odd_core)
     def _():
@@ -574,18 +790,10 @@
         n_wait(lane, owner).wait_recv()
         d_wait(lane, owner).wait_recv()
 
-    def sent(ref, sem):
-        pltpu.make_async_copy(ref, ref, sem).wait()
-
-    sent(gain_ref, gain_send.at[0])
-    for lane in (1, 2):
-        for part in (0, 1):
-            sent(w.at[0, 0:half, :], w_send.at[lane, part])
+    gather_sent()
 
     @pl.when(odd_core)
     def _():
-        for i in range(4):
-            sent(w.at[0, 0:half, :], w_send.at[3, i])
         for layer in range(2):
             for lane in (1, 2, 3):
                 sent(normed.at[0, :, :, 0:share], n_send.at[layer, lane])
@@ -594,10 +802,6 @@
 
         @pl.when(late)
         def _():
-            sent(w.at[0, 0:share, :], w_fwd_send.at[1, 0])
-            for layer in range(2):
-                for lane in (1, 2, 3):
-                    sent(w.at[0, 0:share, :], w_fwd_send.at[layer, lane])
             for i, ref in enumerate([h_in, h_mid, pre.at[0], pre.at[1]]):
                 sent(ref, peer_send.at[i])
             d_wait(0, y).wait_recv()
@@ -622,7 +826,6 @@
 
     @pl.when(even_core)
     def _():
-        sent(w.at[0, 0:share, :], w_fwd_send.at[0, 0])
         n_wait(0, y).wait_recv()
 
         @pl.when(early)
@@ -673,7 +876,7 @@
         ],
         out_specs=pl.BlockSpec((1, share, step), lambda i: (0, 0, i)),
         scratch_shapes=[pltpu.VMEM((share, rows), BF16)],
-        compiler_params=pltpu.CompilerParams(vmem_limit_bytes=32 * 1024 * 1024),
+        compiler_params=pltpu.CompilerParams(vmem_limit_bytes=60 * 1024 * 1024),
         cost_estimate=pl.CostEstimate(
             flops=2 * rows * share * width, bytes_accessed=6 * share * width, transcendentals=0
         ),
@@ -728,6 +931,7 @@
             rows(BF16),
             pltpu.VMEM((count, ROWS, vocab), BF16),
             pltpu.VMEM((ROWS, width), F32),
+            pltpu.VMEM((ROWS, width), BF16),
             pltpu.VMEM((2, ROWS, width), F32),
             pltpu.VMEM((2, ROWS, 128), F32),
             pltpu.VMEM((2, 1, width), F32),
@@ -735,8 +939,8 @@
             pltpu.VMEM((8, 128), F32),
             pltpu.VMEM((4, 8, 128), F32),
             pltpu.VMEM((8, 128), F32),
-            dma((4, 4)),
-            dma((2, 4, 2)),
+            dma((5, 4)),
+            dma((2, 4, 4)),
             dma((2, 4)),
             dma((2, 4)),
             dma((2,)),
@@ -756,6 +960,12 @@
             dma((2,)),
             dma((1,)),
             dma((1,)),
+            pltpu.VMEM((2, 4, 2, share // 8, width), BF16),
+            dma((7, 2)),
+            dma((2, 4, 2)),
+            dma((2, 4, 2)),
+            dma((2, 4, 2)),
+            pltpu.SemaphoreType.REGULAR,
         ],
         compiler_params=pltpu.CompilerParams(
             collective_id=0, has_side_effects=True, vmem_limit_bytes=60 * 1024 * 1024

time: 273 us -> 242 us (0.89); the launches traced: 270 us -> 242 us
  Pallas kernels: 265 us -> 240 us
  local copies, waits for them, and re-layouts: 2.82 us -> 0 us
    pallas_call x1, Pallas kernels: 261 us -> 234 us  [shards(): pl.pallas_call(kernel, name='stack', out_shape=(jax.ShapeDtypeStruct((1,...]
    unnamed x4 -> x0, local copies, waits for them, and re-layouts: 2.82 us -> none
where the time goes in v3:
time: 242 us
  Pallas kernels  240 us (99%)
    pallas_call x1, Pallas kernels, shards(): pl.pallas_call(kernel, name='stack', out_shape=(jax.ShapeDtypeStruct((1,...  234 us
    pallas_call x1, Pallas kernels, product(): pl.pallas_call(product_kernel, name='weight_grad', grid=(width // step,),...  5.75 us

profile of v3, /device:TPU:0, one launch (start us, length us, event | category | flops | bytes accessed | tf_op | source)
XLA Modules:
  0.0 242.1 jit_solution(17355352156649871371)
XLA Ops:
  0.6 233.9 %stack.1 = (f32[1,1]{1,0:T(1,128)}, bf16[4,10,16,512]{3,2,1,0:T(8,128)(2,1)}, bf16[4,10,16,2048]{3,2,1,0:T(8,128)(2,1)}) custom-call(s32[1,8]{1,0:T(1,128)} %lengths_ref.1, s32[8,32]{1,0:T(8,128)} %video_ids_ref.1, s32[8,32]{1,0:T(8,128)} %action_ids_ref.1, s32[8,32]{1,0:T(8,128)} %target_ids_ref.1, f32[1,2048]{1,0:T(1,128)} %gain_ref.1, f32[1,2048]{1,0:T(1,128)} %bitcast.6, ...), custom_call_target="tpu_custom_call" | custom-call | flops 10000000000 | bytes 20000000 | tf_op jit(solution)/shard_map/stack/pallas_call | solution.py:909
  234.6 5.8 %weight_grad.1 = f32[1,512,2048]{2,1,0:T(8,128)} custom-call(bf16[640,512]{1,0:T(8,128)(2,1)} %bitcast.5, bf16[640,2048]{1,0:T(8,128)(2,1)} %bitcast.4), custom_call_target="tpu_custom_call" | custom-call | flops 1342177280 | bytes 6291456 | tf_op jit(solution)/shard_map/weight_grad/pallas_call | solution.py:868

commit v4 on v3

--- a/solution.py
+++ b/solution.py
@@ -11,7 +11,8 @@
 F32 = jnp.float32
 BF16 = jnp.bfloat16
 ROWS = 16
-CUTS = 4
+PIECES = (2, 2, 2, 2)
+CUTS = len(PIECES)
 PRE_SCALE = 0.7978845608028654
 CUBE = 0.044715
 
@@ -60,6 +61,7 @@
     g_in,
     g_out,
     dlog,
+    stats,
     acc,
     raw,
     slope,
@@ -119,7 +121,7 @@
     share = width // 4
     halves = (share * 3 // 8, share // 8)
     main = 2 * halves[0]
-    step = width // CUTS
+    edges = [width * sum(PIECES[:j]) // sum(PIECES) for j in range(CUTS + 1)]
     count = h_in.shape[0]
     vocab = hw.shape[1]
 
@@ -132,6 +134,12 @@
         return pltpu.make_async_remote_copy(
             src_ref=src, dst_ref=dst, send_sem=send, recv_sem=recv, device_id=device, device_id_type=MESH
         )
+
+    def cut(j):
+        return slice(edges[j], edges[j + 1])
+
+    def window(j):
+        return pl.ds(edges[j], edges[j + 1] - edges[j])
 
     barrier = pltpu.get_barrier_semaphore()
     for other in (up, down, far):
@@ -336,11 +344,11 @@
         video_hot = (chosen[0] == lax.broadcasted_iota(jnp.int32, (total, ht.shape[0]), 1)).astype(F32).astype(BF16)
         kinds = actions_ref.shape[0]
         for j in range(CUTS):
-            cols = slice(j * step, (j + 1) * step)
+            cols = cut(j)
             rows = dot(video_hot, ht[:, cols])
             for a in range(kinds):
                 rows = rows + jnp.where(chosen[1] == a, actions_ref[a : a + 1, cols].astype(F32), 0.0)
-            h_in[:, :, cols] = rows.astype(BF16).reshape(count, ROWS, step)
+            h_in[:, :, cols] = rows.astype(BF16).reshape(count, ROWS, -1)
 
     block = min(512, width)
 
@@ -431,7 +439,7 @@
     def _():
         pltpu.make_async_copy(head_ref, hw, local_sem.at[1]).wait()
         for i in range(CUTS):
-            ht[:, i * step : (i + 1) * step] = hw[i * step : (i + 1) * step, :].T
+            ht[:, cut(i)] = hw[cut(i), :].T
 
     def sent(ref, sem):
         pltpu.make_async_copy(ref, ref, sem).wait()
@@ -487,7 +495,7 @@
             sent(w.at[0, 0:share, :], w_fwd_send.at[0, 0])
 
     def h_piece(mb, j):
-        cols = pl.ds(j * step, step)
+        cols = window(j)
         return remote(
             h_out.at[mb, :, cols], h_in.at[mb, :, cols], h_send.at[j], h_recv.at[mb, j], (s + 2, y)
         )
@@ -501,14 +509,11 @@
     def head_copies(mb):
         return [
             remote(ref.at[mb], ref.at[mb], peer_send.at[4 + i], peer_recv.at[4 + i, mb], peer)
-            for i, ref in enumerate([h_out, dlog])
+            for i, ref in enumerate([h_out, dlog, stats])
         ]
 
     def inverse(squares):
         return lax.rsqrt(squares * (1.0 / width) + 1e-05)
-
-    def cut(j):
-        return slice(j * step, (j + 1) * step)
 
     def fold(x):
         return sum(x[:, i : i + 128] for i in range(0, x.shape[1], 128))
@@ -574,7 +579,11 @@
             target = picked_ids[pl.ds(pl.multiple_of(mb * ROWS, ROWS), ROWS), 0:1]
             one_hot = (target == lax.broadcasted_iota(jnp.int32, logits.shape, 1)).astype(F32)
             picked = row_sum(logits * one_hot)
-            dlog[mb] = (exponents / denominator - one_hot).astype(BF16)
+            d = (exponents / denominator - one_hot).astype(BF16)
+            dlog[mb] = d
+            pull = scale * scale * (1.0 / width) * row_sum(d.astype(F32) * logits)
+            stats[mb, 0] = jnp.broadcast_to(scale, stats.shape[2:])
+            stats[mb, 1] = jnp.broadcast_to(pull, stats.shape[2:])
             for copy in head_copies(mb):
                 copy.start()
             losses = jnp.sum(jnp.log(denominator) + top - picked, axis=0, keepdims=True)
@@ -664,7 +673,7 @@
                     turn(layer, owner)
 
     def g_piece(mb, j):
-        cols = pl.ds(j * step, step)
+        cols = window(j)
         return remote(
             g_out.at[mb, :, cols], g_in.at[mb, :, cols], g_send.at[j], g_recv.at[mb, j], (back_target, y)
         )
@@ -687,16 +696,18 @@
         if is_last:
             for copy in head_copies(mb):
                 copy.wait_recv()
-            back = dot(dlog[mb], ht[...]) * out_gain_ref[...]
-            h = h_out[mb].astype(F32)
-            scale = inverse(row_sum(h * h))
-            inner = row_sum(back * h)
-            g_in[mb] = (scale * back - h * (scale * scale * scale * (1.0 / width) * inner)).astype(BF16)
+            scale, pull = stats[mb, 0, :, 0:1], stats[mb, 1, :, 0:1]
+            ahead = dot(dlog[mb], ht[:, cut(0)])
 
         dots = jnp.zeros((ROWS, 128), F32)
         for j in range(CUTS):
             if not is_last:
                 g_piece(mb, j).wait_recv()
+            else:
+                back = ahead * out_gain_ref[:, cut(j)]
+                if j + 1 < CUTS:
+                    ahead = dot(dlog[mb], ht[:, cut(j + 1)])
+                g_in[mb, :, cut(j)] = (scale * back - h_out[mb, :, cut(j)].astype(F32) * pull).astype(BF16)
             d = (g_in[mb, :, cut(j)].astype(F32) * slope[1, :, cut(j)]).astype(BF16)
             dpre[1, mb, :, cut(j)] = d
             dots = dots + fold(d.astype(F32) * pre[1, mb, :, cut(j)])
@@ -815,6 +826,7 @@
         def _():
             sent(h_out, peer_send.at[4])
             sent(dlog, peer_send.at[5])
+            sent(stats, peer_send.at[6])
             for lane in (1, 2, 3):
                 sent(loss_part, part_send.at[lane])
 
@@ -930,6 +942,7 @@
             rows(BF16),
             rows(BF16),
             pltpu.VMEM((count, ROWS, vocab), BF16),
+            pltpu.VMEM((count, 2, ROWS, 128), F32),
             pltpu.VMEM((ROWS, width), F32),
             pltpu.VMEM((ROWS, width), BF16),
             pltpu.VMEM((2, ROWS, width), F32),
@@ -948,8 +961,8 @@
             dma((count, CUTS)),
             dma((CUTS,)),
             dma((count, CUTS)),
-            dma((6,)),
-            dma((6, count)),
+            dma((7,)),
+            dma((7, count)),
             dma((2, 4)),
             dma((4,)),
             dma((2, 4)),

time: 242 us -> 241 us (level)
  no operation moved by 1% of the time
where the time goes in v4:
time: 241 us
  Pallas kernels  238 us (99%)
  between operations  2.41 us (1%)
    pallas_call x1, Pallas kernels, shards(): pl.pallas_call(kernel, name='stack', out_shape=(jax.ShapeDtypeStruct((1,...  232 us
    pallas_call x1, Pallas kernels, product(): pl.pallas_call(product_kernel, name='weight_grad', grid=(width // step,),...  5.75 us

profile of v4, /device:TPU:0, one launch (start us, length us, event | category | flops | bytes accessed | tf_op | source)
XLA Modules:
  0.0 240.6 jit_solution(3669528110482890090)
XLA Ops:
  0.6 232.4 %stack.1 = (f32[1,1]{1,0:T(1,128)}, bf16[4,10,16,512]{3,2,1,0:T(8,128)(2,1)}, bf16[4,10,16,2048]{3,2,1,0:T(8,128)(2,1)}) custom-call(s32[1,8]{1,0:T(1,128)} %lengths_ref.1, s32[8,32]{1,0:T(8,128)} %video_ids_ref.1, s32[8,32]{1,0:T(8,128)} %action_ids_ref.1, s32[8,32]{1,0:T(8,128)} %target_ids_ref.1, f32[1,2048]{1,0:T(1,128)} %gain_ref.1, f32[1,2048]{1,0:T(1,128)} %bitcast.6, ...), custom_call_target="tpu_custom_call" | custom-call | flops 10000000000 | bytes 20000000 | tf_op jit(solution)/shard_map/stack/pallas_call | solution.py:921
  233.1 5.8 %weight_grad.1 = f32[1,512,2048]{2,1,0:T(8,128)} custom-call(bf16[640,512]{1,0:T(8,128)(2,1)} %bitcast.5, bf16[640,2048]{1,0:T(8,128)(2,1)} %bitcast.4), custom_call_target="tpu_custom_call" | custom-call | flops 1342177280 | bytes 6291456 | tf_op jit(solution)/shard_map/weight_grad/pallas_call | solution.py:880

commit v5 on v4

--- a/solution.py
+++ b/solution.py
@@ -548,7 +548,9 @@
         inv_mid = inverse(row_sum(squares))
         squares = jnp.zeros((ROWS, 128), F32)
         for j in range(CUTS):
-            at = (opening if j == 0 else dot(raw[...], w[1, :, cut(j)])) * inv_mid
+            at = opening * inv_mid
+            if j + 1 < CUTS:
+                opening = dot(raw[...], w[1, :, cut(j + 1)])
             result = (h_mid[mb, :, cut(j)].astype(F32) + gelu(at)).astype(BF16)
             h_out[mb, :, cut(j)] = result
             if not is_last:
@@ -738,7 +740,9 @@
             inv = inv_keep[0, :, 0:1]
             pull = inv * inv * (1.0 / width) * row_sum(dots)
             for j in range(CUTS):
-                back = (opening if j == 0 else dot(dpre[0, mb], wt[0, :, cut(j)])) * gains[0, :, cut(j)]
+                back = opening * gains[0, :, cut(j)]
+                if j + 1 < CUTS:
+                    opening = dot(dpre[0, mb], wt[0, :, cut(j + 1)])
                 g_out[mb, :, cut(j)] = (
                     acc[:, cut(j)] + (inv * back - h_in[mb, :, cut(j)].astype(F32) * pull)
                 ).astype(BF16)

time: 241 us -> 233 us (0.967)
  Pallas kernels: 238 us -> 231 us
    pallas_call x1, Pallas kernels: 232 us -> 225 us  [shards(): pl.pallas_call(kernel, name='stack', out_shape=(jax.ShapeDtypeStruct((1,...]
where the time goes in v5:
time: 233 us
  Pallas kernels  231 us (99%)
  between operations  2.41 us (1%)
    pallas_call x1, Pallas kernels, shards(): pl.pallas_call(kernel, name='stack', out_shape=(jax.ShapeDtypeStruct((1,...  225 us
    pallas_call x1, Pallas kernels, product(): pl.pallas_call(product_kernel, name='weight_grad', grid=(width // step,),...  5.75 us

profile of v5, /device:TPU:0, one launch (start us, length us, event | category | flops | bytes accessed | tf_op | source)
XLA Modules:
  0.0 233.1 jit_solution(9785587410577266263)
XLA Ops:
  0.6 224.9 %stack.1 = (f32[1,1]{1,0:T(1,128)}, bf16[4,10,16,512]{3,2,1,0:T(8,128)(2,1)}, bf16[4,10,16,2048]{3,2,1,0:T(8,128)(2,1)}) custom-call(s32[1,8]{1,0:T(1,128)} %lengths_ref.1, s32[8,32]{1,0:T(8,128)} %video_ids_ref.1, s32[8,32]{1,0:T(8,128)} %action_ids_ref.1, s32[8,32]{1,0:T(8,128)} %target_ids_ref.1, f32[1,2048]{1,0:T(1,128)} %gain_ref.1, f32[1,2048]{1,0:T(1,128)} %bitcast.6, ...), custom_call_target="tpu_custom_call" | custom-call | flops 10000000000 | bytes 20000000 | tf_op jit(solution)/shard_map/stack/pallas_call | solution.py:925
  225.6 5.8 %weight_grad.1 = f32[1,512,2048]{2,1,0:T(8,128)} custom-call(bf16[640,512]{1,0:T(8,128)(2,1)} %bitcast.5, bf16[640,2048]{1,0:T(8,128)(2,1)} %bitcast.4), custom_call_target="tpu_custom_call" | custom-call | flops 1342177280 | bytes 6291456 | tf_op jit(solution)/shard_map/weight_grad/pallas_call | solution.py:884

commit v6 on v5

--- a/solution.py
+++ b/solution.py
@@ -635,6 +635,11 @@
     def d_local(layer, mb):
         return pltpu.make_async_copy(dpre.at[layer, mb], dpre_out.at[y, mb], local_sem.at[1])
 
+    def d_whole(layer, owner, lane):
+        return remote(
+            dpre.at[layer], dpre_out.at[y], d_send.at[layer, lane], d_recv.at[lane], (2 * k + layer, owner)
+        )
+
     def d_wait(lane, owner):
         return remote(dpre.at[0], dpre_out.at[owner], d_send.at[0, lane], d_recv.at[lane], peer)
 
@@ -748,8 +753,9 @@
                 ).astype(BF16)
                 g_piece(mb, j).start()
 
-        send_dpre(0, mb)
-        if not is_first:
+        if not is_last:
+            send_dpre(0, mb)
+        if not is_first and not is_last:
             send_dpre(1, mb)
 
         @pl.when(mb < count - 1)
@@ -773,6 +779,11 @@
         @pl.when(last)
         def _():
             lax.fori_loop(0, count, functools.partial(backward_one, is_first=False, is_last=True), 0)
+            for layer in range(2):
+                for lane, owner in lanes:
+                    d_whole(layer, owner, lane).start()
+            d_whole(1, y, 0).start()
+            pltpu.make_async_copy(dpre.at[0], dpre_out.at[y], local_sem.at[1]).start()
 
 
     @pl.when(odd_core)
@@ -869,29 +880,52 @@
                 sent(g_out.at[:, :, cut(j)], g_send.at[j])
 
 
-def product_kernel(normed_ref, dpre_ref, out_ref, turned):
-    @pl.when(pl.program_id(0) == 0)
-    def _():
-        turned[...] = normed_ref[...].T
-
-    out_ref[0] = dot(turned[...], dpre_ref[...])
+def product_kernel(normed_ref, dpre_ref, out_ref, lefts, right, results, left_sem, right_sem, out_sem):
+    parts, step = lefts.shape[0], lefts.shape[2]
+    loads = [
+        pltpu.make_async_copy(normed_ref.at[:, pl.ds(i * step, step)], lefts.at[i], left_sem.at[i])
+        for i in range(parts)
+    ]
+    whole = pltpu.make_async_copy(dpre_ref, right, right_sem)
+    loads[0].start()
+    whole.start()
+    for load in loads[1:]:
+        load.start()
+    stores = []
+    for i in range(parts):
+        loads[i].wait()
+        turned = lefts[i].T
+        if i == 0:
+            whole.wait()
+        results[i] = dot(turned, right[...])
+        stores.append(
+            pltpu.make_async_copy(results.at[i], out_ref.at[0, pl.ds(i * step, step), :], out_sem.at[i])
+        )
+        stores[-1].start()
+    for store in stores:
+        store.wait()
 
 
 def product(normed, dpre):
     rows, share = normed.shape
     width = dpre.shape[1]
-    step = min(512, width)
+    step = min(256, share)
+    parts = share // step
+    hbm = pl.BlockSpec(memory_space=pl.ANY)
     return pl.pallas_call(
         product_kernel,
         name="weight_grad",
-        grid=(width // step,),
         out_shape=jax.ShapeDtypeStruct((1, share, width), F32),
-        in_specs=[
-            pl.BlockSpec((rows, share), lambda i: (0, 0)),
-            pl.BlockSpec((rows, step), lambda i: (0, i)),
+        in_specs=[hbm, hbm],
+        out_specs=hbm,
+        scratch_shapes=[
+            pltpu.VMEM((parts, rows, step), BF16),
+            pltpu.VMEM((rows, width), BF16),
+            pltpu.VMEM((parts, step, width), F32),
+            pltpu.SemaphoreType.DMA((parts,)),
+            pltpu.SemaphoreType.DMA,
+            pltpu.SemaphoreType.DMA((parts,)),
         ],
-        out_specs=pl.BlockSpec((1, share, step), lambda i: (0, 0, i)),
-        scratch_shapes=[pltpu.VMEM((share, rows), BF16)],
         compiler_params=pltpu.CompilerParams(vmem_limit_bytes=60 * 1024 * 1024),
         cost_estimate=pl.CostEstimate(
             flops=2 * rows * share * width, bytes_accessed=6 * share * width, transcendentals=0

time: 233 us -> 233 us (level)
  no operation moved by 1% of the time
where the time goes in v6:
time: 233 us; the launch traced here: 232 us
  Pallas kernels  230 us (99%)
  between operations  2.41 us (1%)
    pallas_call x1, Pallas kernels, shards(): pl.pallas_call(kernel, name='stack', out_shape=(jax.ShapeDtypeStruct((1,...  225 us
    pallas_call x1, Pallas kernels, product(): pl.pallas_call(product_kernel, name='weight_grad', out_shape=jax.ShapeDty...  5.2 us

profile of v6, /device:TPU:0, one launch (start us, length us, event | category | flops | bytes accessed | tf_op | source)
XLA Modules:
  0.0 232.4 jit_solution(11623148885113045704)
XLA Ops:
  0.6 224.8 %stack.1 = (f32[1,1]{1,0:T(1,128)}, bf16[4,10,16,512]{3,2,1,0:T(8,128)(2,1)}, bf16[4,10,16,2048]{3,2,1,0:T(8,128)(2,1)}) custom-call(s32[1,8]{1,0:T(1,128)} %lengths_ref.1, s32[8,32]{1,0:T(8,128)} %video_ids_ref.1, s32[8,32]{1,0:T(8,128)} %action_ids_ref.1, s32[8,32]{1,0:T(8,128)} %target_ids_ref.1, f32[1,2048]{1,0:T(1,128)} %gain_ref.1, f32[1,2048]{1,0:T(1,128)} %bitcast.6, ...), custom_call_target="tpu_custom_call" | custom-call | flops 10000000000 | bytes 20000000 | tf_op jit(solution)/shard_map/stack/pallas_call | solution.py:959
  225.4 5.2 %weight_grad.1 = f32[1,512,2048]{2,1,0:T(8,128)} custom-call(bf16[640,512]{1,0:T(8,128)(2,1)} %bitcast.5, bf16[640,2048]{1,0:T(8,128)(2,1)} %bitcast.4), custom_call_target="tpu_custom_call" | custom-call | flops 1342177280 | bytes 6291456 | tf_op jit(solution)/shard_map/weight_grad/pallas_call | solution.py:915

commit v7 on v6

--- a/solution.py
+++ b/solution.py
@@ -520,12 +520,13 @@
 
     def forward_one(mb, carry, is_first, is_last):
         squares = jnp.zeros((ROWS, 128), F32)
-        for j in range(CUTS):
+        for j in range(1 if is_first else CUTS):
             if not is_first:
                 h_piece(mb, j).wait_recv()
-            h = h_in[mb, :, cut(j)].astype(F32)
+            taken = slice(0, width) if is_first else cut(j)
+            h = h_in[mb, :, taken].astype(F32)
             squares = squares + fold(h * h)
-            product = dot((h * gains[0, :, cut(j)]).astype(BF16), w[0, cut(j), :])
+            product = dot((h * gains[0, :, taken]).astype(BF16), w[0, taken, :])
             if j == 0:
                 acc[...] = product
             else:
@@ -558,13 +559,17 @@
             pre[1, mb, :, cut(j)] = at
             wide = result.astype(F32)
             squares = squares + fold(wide * wide)
-        for j in range(CUTS):
-            normed[0, mb, :, cut(j)] = (
-                h_in[mb, :, cut(j)].astype(F32) * inv * gains[0, :, cut(j)]
-            ).astype(BF16)
-            normed[1, mb, :, cut(j)] = (
-                h_mid[mb, :, cut(j)].astype(F32) * inv_mid * gains[1, :, cut(j)]
-            ).astype(BF16)
+        def keep_normed():
+            for j in range(CUTS):
+                normed[0, mb, :, cut(j)] = (
+                    h_in[mb, :, cut(j)].astype(F32) * inv * gains[0, :, cut(j)]
+                ).astype(BF16)
+                normed[1, mb, :, cut(j)] = (
+                    h_mid[mb, :, cut(j)].astype(F32) * inv_mid * gains[1, :, cut(j)]
+                ).astype(BF16)
+
+        if not is_last:
+            keep_normed()
 
         @pl.when(late)
         def _():
@@ -590,6 +595,7 @@
                 copy.start()
             losses = jnp.sum(jnp.log(denominator) + top - picked, axis=0, keepdims=True)
             loss_part[...] += jnp.broadcast_to(losses, loss_part.shape)
+            keep_normed()
 
         return carry
 

time: 233 us -> 233 us (level)
  no operation moved by 1% of the time
where the time goes in v7:
time: 233 us
  Pallas kernels  230 us (99%)
  between operations  2.41 us (1%)
    pallas_call x1, Pallas kernels, shards(): pl.pallas_call(kernel, name='stack', out_shape=(jax.ShapeDtypeStruct((1,...  225 us
    pallas_call x1, Pallas kernels, product(): pl.pallas_call(product_kernel, name='weight_grad', out_shape=jax.ShapeDty...  5.2 us

profile of v7, /device:TPU:0, one launch (start us, length us, event | category | flops | bytes accessed | tf_op | source)
XLA Modules:
  0.0 232.6 jit_solution(11453051000000869856)
XLA Ops:
  0.6 225.0 %stack.1 = (f32[1,1]{1,0:T(1,128)}, bf16[4,10,16,512]{3,2,1,0:T(8,128)(2,1)}, bf16[4,10,16,2048]{3,2,1,0:T(8,128)(2,1)}) custom-call(s32[1,8]{1,0:T(1,128)} %lengths_ref.1, s32[8,32]{1,0:T(8,128)} %video_ids_ref.1, s32[8,32]{1,0:T(8,128)} %action_ids_ref.1, s32[8,32]{1,0:T(8,128)} %target_ids_ref.1, f32[1,2048]{1,0:T(1,128)} %gain_ref.1, f32[1,2048]{1,0:T(1,128)} %bitcast.6, ...), custom_call_target="tpu_custom_call" | custom-call | flops 10000000000 | bytes 20000000 | tf_op jit(solution)/shard_map/stack/pallas_call | solution.py:965
  225.7 5.2 %weight_grad.1 = f32[1,512,2048]{2,1,0:T(8,128)} custom-call(bf16[640,512]{1,0:T(8,128)(2,1)} %bitcast.5, bf16[640,2048]{1,0:T(8,128)(2,1)} %bitcast.4), custom_call_target="tpu_custom_call" | custom-call | flops 1342177280 | bytes 6291456 | tf_op jit(solution)/shard_map/weight_grad/pallas_call | solution.py:921
